TPU v7x, 512 devices: a whole 4x4x16 slice. The times are simulated.
512 devices in a mesh: stream: 16 (over z), tile: 4 (over y_lo, core), band: 8 (over y_hi, x).
Axes of the slice: x: 4, y: 4 (y_hi: 2, y_lo: 2; y = y_hi * 2 + y_lo), z: 16, core: 2. Of those that a mesh axis runs over, the one named last changes fastest.
Arguments:
- latents: bfloat16 [384, 8, 512, 256], P('stream', 'band', 'tile'), may hold values from -6 to 6
- owners: int32 [384, 1], P('stream'), may hold values from 0 to 15; in each aligned block of 24 rows (0 to 23, 24 to 47, ...) at most 2 rows name the same one
- live_counts: int32 [16], P('stream'), may hold values from 12 to 24, as said below
- spatial_weight: bfloat16 [3, 3, 256, 256], replicated, may hold values from -0.125 to 0.125
- temporal_weight: bfloat16 [3, 256, 256], replicated, may hold values from -0.21875 to 0.21875
- out_weight: bfloat16 [3, 256], replicated, may hold values from -0.375 to 0.375
Outputs:
- frames: float32 [512, 8, 3, 512], P('stream', 'band', None, 'tile')
Inputs may be any that keep to these rules, and one draw needn't show every extreme that they name: `owners`: among the 24 groups of one source device no owner is named more than 2 times, a bound that some block reaches. `live_counts`: some source device has all 24 groups live in every draw.
All inputs are finite; a program needn't handle non-finite values.
Results may differ from a plain program's by a relative error of at most 0.0031.
Values may be sent and summed in bfloat16 or wider, within the bound.
No kernel may reach another device: no remote copies, remote signals or barrier semaphores. Data moves between devices by JAX's collectives and lax.ppermute only.
A program may use at most 128 MiB of HBM per device.

v0:
```python
import jax
import jax.numpy as jnp
from jax import lax
from jax.sharding import PartitionSpec as P

FC = 2
TH = 16
TW = 4


def with_halo(cells, sides, width):
    for axis, dim in sides:
        count = lax.axis_size(axis)
        ends = count - 1
        head = lax.slice_in_dim(cells, 0, width, axis=dim)
        tail = lax.slice_in_dim(cells, cells.shape[dim] - width, cells.shape[dim], axis=dim)
        cells = jnp.concatenate(
            [
                lax.ppermute(tail, axis, [(i, (i + 1) % count) for i in range(ends)]),
                cells,
                lax.ppermute(head, axis, [((i + 1) % count, i) for i in range(ends)]),
            ],
            axis=dim,
        )
    return cells


def swapped(value, axis, distance):
    return lax.ppermute(value, axis, [(i, i ^ 1 << distance) for i in range(lax.axis_size(axis))])


def decode_items(blocks, spatial_weight, temporal_weight, out_weight):
    item_count = blocks.shape[0]
    channel_count = blocks.shape[-1]
    grid_field = blocks.reshape(item_count, FC, TH, TW, channel_count)
    rimmed = with_halo(grid_field, (("tile", 2),), 1)
    padded = jnp.pad(rimmed, ((0, 0), (0, 0), (0, 0), (1, 1), (0, 0)))
    spatial = jnp.zeros((item_count, FC, TH, TW, channel_count), jnp.float32)
    for row_tap in range(3):
        for col_tap in range(3):
            window = padded[:, :, row_tap : row_tap + TH, col_tap : col_tap + TW, :]
            spatial = spatial + jnp.einsum(
                "bfhwc,cd->bfhwd",
                window,
                spatial_weight[row_tap, col_tap],
                preferred_element_type=jnp.float32,
            )
    activated = jax.nn.silu(spatial).astype(jnp.bfloat16)
    framed = jnp.pad(activated, ((0, 0), (1, 1), (0, 0), (0, 0), (0, 0)))
    temporal = grid_field.astype(jnp.float32)
    for time_tap in range(3):
        temporal = temporal + jnp.einsum(
            "bfhwc,cd->bfhwd",
            framed[:, time_tap : time_tap + FC],
            temporal_weight[time_tap],
            preferred_element_type=jnp.float32,
        )
    mixed_out = temporal.astype(jnp.bfloat16)
    pixels = jnp.einsum(
        "oc,bfhwc->bofhw", out_weight, mixed_out, preferred_element_type=jnp.float32
    )
    return pixels.reshape(item_count, 3, FC * TH * TW)


def inverse_haar(values):
    root_half = 0.5**0.5
    band_count = lax.axis_size("band")
    band_bits = band_count.bit_length() - 1
    for section_bit in range(band_bits):
        partner = swapped(values, "band", section_bit)
        high_bit = lax.axis_index("band") >> section_bit & 1
        values = jnp.where(high_bit == 0, values + partner, partner - values) * root_half
    return values


def local(latents, owners, live_counts, spatial_weight, temporal_weight, out_weight):
    group_count = latents.shape[0]
    band_local = latents.shape[1]
    cell_count = latents.shape[2]
    channel_count = latents.shape[3]
    stream_count = lax.axis_size("stream")
    slot_most = max(2, (group_count + stream_count - 1) // stream_count)
    owner_list = owners[:, 0]
    positions = jnp.arange(group_count, dtype=jnp.int32)
    same_owner = owner_list[:, None] == owner_list[None, :]
    earlier_mask = positions[:, None] < positions[None, :]
    slot_rank = jnp.sum((same_owner & earlier_mask).astype(jnp.int32), axis=0)
    is_valid = positions < live_counts[0]
    targets = jnp.arange(stream_count * slot_most, dtype=jnp.int32)
    placing = (
        (targets[:, None] // slot_most == owner_list[None, :])
        & (targets[:, None] % slot_most == slot_rank[None, :])
        & is_valid[None, :]
    )
    pixels = decode_items(
        latents.reshape(group_count * band_local, cell_count, channel_count),
        spatial_weight,
        temporal_weight,
        out_weight,
    )
    transformed = inverse_haar(pixels.reshape(group_count, band_local, 3, cell_count))
    outgoing = jnp.einsum(
        "rj,jsok->rsok", placing.astype(jnp.float32), transformed, precision=lax.Precision.HIGHEST
    )
    return lax.all_to_all(outgoing, "stream", split_axis=0, concat_axis=0, tiled=True)


def solution(mesh):
    return jax.shard_map(
        local,
        mesh=mesh,
        in_specs=(P("stream", "band", "tile", None), P("stream", None), P("stream"), P(), P(), P()),
        out_specs=P("stream", "band", None, "tile"),
        check_vma=False,
    )
```

profile of v0, /device:TPU:1, one launch (start us, length us, event | category | flops | bytes accessed | tf_op | source)
XLA Modules:
  0.0 99.4 jit_solution(4963182395364336671)
XLA Ops:
  0.0 2.4 %copy.46 = bf16[24,1,128,256]{3,0,2,1:T(8,128)(2,1)S(1)} copy(bf16[24,1,128,256]{3,2,1,0:T(8,128)(2,1)} %param.6) | data formatting | bytes 3145728 | tf_op args[0]
  2.4 0.9 copy.47
  3.3 0.3 fusion.80
  3.6 4.6 %collective-permute-start = (bf16[24,2,1,4,256]{4,2,3,1,0:T(2,128)(2,1)S(1)}, bf16[24,2,1,4,256]{4,2,3,1,0:T(2,128)(2,1)S(1)}, u32[]{:S(2)}, u32[]{:S(2)}) collective-permute-start(bf16[24,2,1,4,256]{4,2,3,1,0:T(2,128)(2,1)S(1)} %get-tuple-element.7), channel_id=1, source_target_pairs={{0,8},{8,16},{16,24},{1,9},{9,17},{17,25},{2,10},{10,18},{18,26},{... | collective-permute-start | bytes 294920 | tf_op jit(solution)/shard_map/ppermute | solution.py:19
  8.2 5.5 %collective-permute-start.1 = (bf16[24,2,1,4,256]{4,2,3,1,0:T(2,128)(2,1)S(1)}, bf16[24,2,1,4,256]{4,2,3,1,0:T(2,128)(2,1)S(1)}, u32[]{:S(2)}, u32[]{:S(2)}) collective-permute-start(bf16[24,2,1,4,256]{4,2,3,1,0:T(2,128)(2,1)S(1)} %get-tuple-element.8), channel_id=1, source_target_pairs={{8,0},{16,8},{24,16},{9,1},{17,9},{25,17},{10,2},{18,10},{26,18},{... | collective-permute-start | bytes 294920 | tf_op jit(solution)/shard_map/ppermute | solution.py:21
  13.7 1.8 %fusion.48 = f32[24,2,16,4,256]{4,2,3,1,0:T(8,128)S(1)} fusion(bf16[3,3,256,256]{3,2,1,0:T(8,128)(2,1)S(1)} %copy-done.1, bf16[24,2,16,4,256]{4,0,3,2,1:T(8,128)(2,1)S(1)} %bitcast.106), kind=kOutput, calls=%fused_computation.52 | convolution fusion | flops 402653184 | bytes 4849664 | tf_op jit(solution)/shard_map/bfhwc,cd->bfhwd/dot_general | solution.py:42
  15.6 1.8 %fusion.5 = bf16[24,2,18,6,256]{4,2,3,1,0:T(8,128)(2,1)S(1)} fusion(bf16[24,2,1,4,256]{4,2,3,1,0:T(2,128)(2,1)S(1)} %collective-permute-done.1, bf16[24,2,16,4,256]{4,2,3,1,0:T(8,128)(2,1)S(1)} %copy.47, bf16[24,2,1,4,256]{4,2,3,1,0:T(2,128)(2,1)S(1)} %collective-permute-done), kind=kLoop, calls=%fused_computation.9 | loop fusion | flops 15925248 | bytes 4423680 | tf_op jit(solution)/shard_map/concatenate | solution.py:17
  17.3 0.6 fusion.10
  17.9 0.6 fusion.12
  18.5 0.6 fusion.14
  19.1 2.3 %fusion.16 = f32[24,2,16,4,256]{4,2,3,1,0:T(8,128)} fusion(bf16[24,2,18,6,256]{4,2,3,1,0:T(8,128)(2,1)S(1)} %fusion.5, bf16[3,3,256,256]{3,2,1,0:T(8,128)(2,1)S(1)} %copy-done.1), kind=kOutput, calls=%fused_computation.23 | convolution fusion | flops 402653184 | bytes 4849664 | tf_op jit(solution)/shard_map/bfhwc,cd->bfhwd/dot_general | solution.py:42
  21.4 2.3 %fusion.20 = f32[24,2,16,4,256]{4,2,3,1,0:T(8,128)} fusion(bf16[24,2,18,6,256]{4,2,3,1,0:T(8,128)(2,1)S(1)} %fusion.5, bf16[3,3,256,256]{3,2,1,0:T(8,128)(2,1)S(1)} %copy-done.1), kind=kOutput, calls=%fused_computation.28 | convolution fusion | flops 402653184 | bytes 4849664 | tf_op jit(solution)/shard_map/bfhwc,cd->bfhwd/dot_general | solution.py:42
  23.6 2.4 %fusion.18 = f32[24,2,16,4,256]{4,2,3,1,0:T(8,128)} fusion(bf16[24,2,16,4,256]{4,2,3,1,0:T(8,128)(2,1)S(1)} %copy.47, bf16[24,2,1,4,256]{4,2,3,1,0:T(2,128)(2,1)S(1)} %collective-permute-done, bf16[3,3,256,256]{3,2,1,0:T(8,128)(2,1)S(1)} %copy-done.1), kind=kOutput, calls=%fused_computation.26 | convolution fusion | flops 405798912 | bytes 5046272 | tf_op jit(solution)/shard_map/bfhwc,cd->bfhwd/dot_general | solution.py:42
  26.0 2.4 %fusion.8 = f32[24,2,16,4,256]{4,2,3,1,0:T(8,128)} fusion(bf16[24,2,1,4,256]{4,2,3,1,0:T(2,128)(2,1)S(1)} %collective-permute-done.1, bf16[24,2,16,4,256]{4,2,3,1,0:T(8,128)(2,1)S(1)} %copy.47, bf16[3,3,256,256]{3,2,1,0:T(8,128)(2,1)S(1)} %copy-done.1), kind=kOutput, calls=%fused_computation.15 | convolution fusion | flops 405798912 | bytes 5046272 | tf_op jit(solution)/shard_map/bfhwc,cd->bfhwd/dot_general | solution.py:42
  28.4 5.8 %multiply_convert_fusion = bf16[24,2,16,4,256]{4,2,3,1,0:T(8,128)(2,1)S(1)} fusion(f32[24,2,16,4,256]{4,2,3,1,0:T(8,128)} %fusion.8, f32[24,2,16,4,256]{4,2,3,1,0:T(8,128)S(1)} %fusion.10, f32[24,2,16,4,256]{4,2,3,1,0:T(8,128)S(1)} %fusion.12, f32[24,2,16,4,256]{4,2,3,1,0:T(8,128)S(1)} %fusion.48, f32[24,2,16,4,256]{4,2,3,1,0:T(8,128)S(1)} %fusion.14, ...), kind=kOutput, calls=%fused_computation.11 | convolution fusion | flops 412876800 | bytes 28442624 | tf_op jit(solution)/shard_map/bfhwc,cd->bfhwd/dot_general | solution.py:42
  34.2 0.4 pad_slice_fusion
  34.6 0.6 copy-done.2
  35.2 3.8 %fusion.23 = f32[24,2,16,4,256]{4,0,3,2,1:T(8,128)} fusion(bf16[24,2,16,4,256]{4,2,3,1,0:T(8,128)(2,1)S(1)} %multiply_convert_fusion, bf16[3,256,256]{2,1,0:T(8,128)(2,1)S(1)} %copy-done.2), kind=kOutput, calls=%fused_computation.31 | convolution fusion | flops 402653184 | bytes 4849664 | tf_op jit(solution)/shard_map/bfhwc,cd->bfhwd/dot_general | solution.py:52
  39.0 3.9 %fusion.25 = f32[24,2,16,4,256]{4,0,3,2,1:T(8,128)} fusion(bf16[24,2,16,4,256]{4,2,3,1,0:T(8,128)(2,1)S(1)} %get-tuple-element.6, bf16[3,256,256]{2,1,0:T(8,128)(2,1)S(1)} %copy-done.2), kind=kOutput, calls=%fused_computation.33 | convolution fusion | flops 402653184 | bytes 4849664 | tf_op jit(solution)/shard_map/bfhwc,cd->bfhwd/dot_general | solution.py:52
  42.9 6.1 %fusion.32 = f32[24,3,2,16,4]{0,1,4,3,2:T(4,128)S(1)} fusion(f32[24,2,16,4,256]{4,0,3,2,1:T(8,128)} %fusion.23, f32[24,2,16,4,256]{4,0,3,2,1:T(8,128)} %fusion.25, bf16[24,2,16,4,256]{4,0,3,2,1:T(8,128)(2,1)S(1)} %bitcast.107, bf16[24,2,16,4,256]{4,2,3,1,0:T(8,128)(2,1)S(1)} %get-tuple-element.5, bf16[3,256,256]{2,1,0:T(8,128)(2,1)} %param.10, ...), kind=kOutput, calls=%fused_computation.36 | convolution fusion | flops 411303936 | bytes 9606656 | tf_op jit(solution)/shard_map/oc,bfhwc->bofhw/dot_general | solution.py:59
  49.0 0.1 copy.56
  49.1 2.7 %collective-permute-start.2 = (f32[24,1,3,128]{0,3,2,1:T(8,128)S(1)}, f32[24,1,3,128]{0,3,2,1:T(8,128)S(1)}, u32[]{:S(2)}, u32[]{:S(2)}) collective-permute-start(f32[24,1,3,128]{0,3,2,1:T(8,128)S(1)} %bitcast.108), channel_id=1, source_target_pairs={{0,1},{1,0},{2,3},{3,2},{4,5},{5,4},{6,7},{7,6},{8,9},{9,8},{10,11... | collective-permute-start | bytes 110600 | tf_op jit(solution)/shard_map/ppermute | solution.py:29
  51.9 0.1 convert_reduce_fusion
  51.9 6.0 %collective-permute-done.2 = f32[24,1,3,128]{0,3,2,1:T(8,128)S(1)} collective-permute-done((f32[24,1,3,128]{0,3,2,1:T(8,128)S(1)}, f32[24,1,3,128]{0,3,2,1:T(8,128)S(1)}, u32[]{:S(2)}, u32[]{:S(2)}) %collective-permute-start.2) | collective-permute-done | bytes 36896 | tf_op jit(solution)/shard_map/ppermute | solution.py:29
  58.0 1.9 %collective-permute-start.3 = (f32[24,1,3,128]{0,3,2,1:T(8,128)S(1)}, f32[24,1,3,128]{0,3,2,1:T(8,128)S(1)}, u32[]{:S(2)}, u32[]{:S(2)}) collective-permute-start(f32[24,1,3,128]{0,3,2,1:T(8,128)S(1)} %select_multiply_fusion.1), channel_id=1, source_target_pairs={{0,2},{1,3},{2,0},{3,1},{4,6},{5,7},{6,4},{7,5},{8,10},{9,11},{10,... | collective-permute-start | bytes 110600 | tf_op jit(solution)/shard_map/ppermute | solution.py:29
  60.5 6.9 %collective-permute-done.3 = f32[24,1,3,128]{0,3,2,1:T(8,128)S(1)} collective-permute-done((f32[24,1,3,128]{0,3,2,1:T(8,128)S(1)}, f32[24,1,3,128]{0,3,2,1:T(8,128)S(1)}, u32[]{:S(2)}, u32[]{:S(2)}) %collective-permute-start.3) | collective-permute-done | bytes 36896 | tf_op jit(solution)/shard_map/ppermute | solution.py:29
  67.5 1.9 %collective-permute-start.4 = (f32[24,1,3,128]{0,3,2,1:T(8,128)S(1)}, f32[24,1,3,128]{0,3,2,1:T(8,128)S(1)}, u32[]{:S(2)}, u32[]{:S(2)}) collective-permute-start(f32[24,1,3,128]{0,3,2,1:T(8,128)S(1)} %select_multiply_fusion), channel_id=1, source_target_pairs={{0,4},{1,5},{2,6},{3,7},{4,0},{5,1},{6,2},{7,3},{8,12},{9,13},{10,... | collective-permute-start | bytes 110600 | tf_op jit(solution)/shard_map/ppermute | solution.py:29
  69.4 6.6 %collective-permute-done.4 = f32[24,1,3,128]{0,3,2,1:T(8,128)S(1)} collective-permute-done((f32[24,1,3,128]{0,3,2,1:T(8,128)S(1)}, f32[24,1,3,128]{0,3,2,1:T(8,128)S(1)}, u32[]{:S(2)}, u32[]{:S(2)}) %collective-permute-start.4) | collective-permute-done | bytes 36896 | tf_op jit(solution)/shard_map/ppermute | solution.py:29
  76.0 0.3 convolution_bitcast_fusion
  76.4 0.1 copy.58
  76.4 22.3 %all_to_all.5 = f32[32,1,3,128]{3,1,2,0:T(1,128)S(1)} all-to-all(f32[32,1,3,128]{3,1,2,0:T(1,128)S(1)} %copy.58), channel_id=1, replica_groups=mesh['stream'=16,'tile'=4,'band'=8] {'stream'}, dimensions={0} | all-to-all | bytes 98304 | tf_op jit(solution)/shard_map/all_to_all | solution.py:105
  98.7 0.6 copy.87
  (13 shorter events, 0.1 us)
Async XLA Ops:
  0.0 42.9 %copy-start = (bf16[3,256]{1,0:T(4,128)(2,1)S(1)}, bf16[3,256]{1,0:T(4,128)(2,1)}, u32[]{:S(2)}) copy-start(bf16[3,256]{1,0:T(4,128)(2,1)} %param.11) | copy-start | bytes 4612
  0.0 13.7 %copy-start.1 = (bf16[3,3,256,256]{3,2,1,0:T(8,128)(2,1)S(1)}, bf16[3,3,256,256]{3,2,1,0:T(8,128)(2,1)}, u32[]{:S(2)}) copy-start(bf16[3,3,256,256]{3,2,1,0:T(8,128)(2,1)} %param.9) | copy-start | bytes 3538948
  3.6 12.0 %collective-permute-start = (bf16[24,2,1,4,256]{4,2,3,1,0:T(2,128)(2,1)S(1)}, bf16[24,2,1,4,256]{4,2,3,1,0:T(2,128)(2,1)S(1)}, u32[]{:S(2)}, u32[]{:S(2)}) collective-permute-start(bf16[24,2,1,4,256]{4,2,3,1,0:T(2,128)(2,1)S(1)} %get-tuple-element.7), channel_id=1, source_target_pairs={{0,8},{8,16},{16,24},{1,9},{9,17},{17,25},{2,10},{10,18},{18,26},{... | collective-permute-start | bytes 294920 | tf_op jit(solution)/shard_map/ppermute | solution.py:19
  8.2 7.4 %collective-permute-start.1 = (bf16[24,2,1,4,256]{4,2,3,1,0:T(2,128)(2,1)S(1)}, bf16[24,2,1,4,256]{4,2,3,1,0:T(2,128)(2,1)S(1)}, u32[]{:S(2)}, u32[]{:S(2)}) collective-permute-start(bf16[24,2,1,4,256]{4,2,3,1,0:T(2,128)(2,1)S(1)} %get-tuple-element.8), channel_id=1, source_target_pairs={{8,0},{16,8},{24,16},{9,1},{17,9},{25,17},{10,2},{18,10},{26,18},{... | collective-permute-start | bytes 294920 | tf_op jit(solution)/shard_map/ppermute | solution.py:21
  34.2 1.0 %copy-start.2 = (bf16[3,256,256]{2,1,0:T(8,128)(2,1)S(1)}, bf16[3,256,256]{2,1,0:T(8,128)(2,1)}, u32[]{:S(2)}) copy-start(bf16[3,256,256]{2,1,0:T(8,128)(2,1)} %param.10) | copy-start | bytes 1179652
  42.9 8.9 %copy-start.3 = (s32[24,1]{0,1:T(1,128)S(1)}, s32[24,1]{0,1:T(1,128)}, u32[]{:S(2)}) copy-start(s32[24,1]{0,1:T(1,128)} %param.7) | copy-start | bytes 292
  49.1 8.8 %collective-permute-start.2 = (f32[24,1,3,128]{0,3,2,1:T(8,128)S(1)}, f32[24,1,3,128]{0,3,2,1:T(8,128)S(1)}, u32[]{:S(2)}, u32[]{:S(2)}) collective-permute-start(f32[24,1,3,128]{0,3,2,1:T(8,128)S(1)} %bitcast.108), channel_id=1, source_target_pairs={{0,1},{1,0},{2,3},{3,2},{4,5},{5,4},{6,7},{7,6},{8,9},{9,8},{10,11... | collective-permute-start | bytes 110600 | tf_op jit(solution)/shard_map/ppermute | solution.py:29
  58.0 9.5 %collective-permute-start.3 = (f32[24,1,3,128]{0,3,2,1:T(8,128)S(1)}, f32[24,1,3,128]{0,3,2,1:T(8,128)S(1)}, u32[]{:S(2)}, u32[]{:S(2)}) collective-permute-start(f32[24,1,3,128]{0,3,2,1:T(8,128)S(1)} %select_multiply_fusion.1), channel_id=1, source_target_pairs={{0,2},{1,3},{2,0},{3,1},{4,6},{5,7},{6,4},{7,5},{8,10},{9,11},{10,... | collective-permute-start | bytes 110600 | tf_op jit(solution)/shard_map/ppermute | solution.py:29
  67.5 8.6 %collective-permute-start.4 = (f32[24,1,3,128]{0,3,2,1:T(8,128)S(1)}, f32[24,1,3,128]{0,3,2,1:T(8,128)S(1)}, u32[]{:S(2)}, u32[]{:S(2)}) collective-permute-start(f32[24,1,3,128]{0,3,2,1:T(8,128)S(1)} %select_multiply_fusion), channel_id=1, source_target_pairs={{0,4},{1,5},{2,6},{3,7},{4,0},{5,1},{6,2},{7,3},{8,12},{9,13},{10,... | collective-permute-start | bytes 110600 | tf_op jit(solution)/shard_map/ppermute | solution.py:29
where the time goes:
time: 101 us; the launch traced here: 99.4 us
  matrix products  32.8 us (32%)
  blocking collectives  22.3 us (22%)
  waiting for transfers between devices  19.5 us (19%)
  starting transfers between devices  16.7 us (17%)
  local copies, waits for them, and re-layouts  5.32 us (5%)
  other arithmetic  1.92 us (2%)
    all_to_all x1, blocking collectives, local(): lax.all_to_all(outgoing, 'stream', split_axis=0, concat_axis=0, tiled=True)  22.3 us
    ppermute x3, waiting for transfers between devices, swapped(): lax.ppermute(value, axis, [(i, i ^ 1 << distance) for i in range(lax.axis...  19.5 us
    dot_general x9, matrix products, decode_items(): jnp.einsum('bfhwc,cd->bfhwd', window, spatial_weight[row_tap, col_tap], p...  18.7 us
    dot_general x2, matrix products, decode_items(): jnp.einsum('bfhwc,cd->bfhwd', framed[:, time_tap:time_tap + FC], temporal...  7.69 us
    ppermute x3, starting transfers between devices, swapped(): lax.ppermute(value, axis, [(i, i ^ 1 << distance) for i in range(lax.axis...  6.56 us
    dot_general x1, matrix products, decode_items(): jnp.einsum('oc,bfhwc->bofhw', out_weight, mixed_out, preferred_element_ty...  6.11 us
    ppermute x1, starting transfers between devices, with_halo(): lax.ppermute(head, axis, [((i + 1) % count, i) for i in range(ends)])  5.49 us
    ppermute x1, starting transfers between devices, with_halo(): lax.ppermute(tail, axis, [(i, (i + 1) % count) for i in range(ends)])  4.59 us
  transfers between devices with their start and end apart: 5, of which 3 were waited for; matrix products, arithmetic and copies ran while one was open for 2% of the time, Pallas kernels for 0%

commit v1 on v0

v1 whole, which is shorter than its diff:
```python
import jax
import jax.numpy as jnp
from jax import lax
from jax.experimental import pallas as pl
from jax.experimental.pallas import tpu as pltpu
from jax.sharding import PartitionSpec as P

C = 256
FC = 2
TH = 16
TW = 4
GB = 8
GF = FC * GB
CELLS = FC * TH * TW
BF = jnp.bfloat16
F32 = jnp.float32


def one_hot_rows(size, order):
    rows = lax.broadcasted_iota(jnp.int32, (size, size), 0)
    cols = lax.broadcasted_iota(jnp.int32, (size, size), 1)
    return (order(rows) == cols).astype(F32).astype(BF)


def dot(a, b):
    return lax.dot_general(a, b, (((1,), (0,)), ((), ())), preferred_element_type=F32)


def silu(x):
    return 0.5 * x * (1.0 + jnp.tanh(0.5 * x))


def decode_kernel(
    even_ref, live_ref, x_ref, side_a_ref, side_b_ref, ws_ref, wt_ref, wo_ref, owners_ref,
    out_ref, xt, perm, perm_side, proj, pix,
):
    step = pl.program_id(0)

    @pl.when(step == 0)
    def _():
        perm[...] = one_hot_rows(
            256, lambda r: (r & 7) * 32 + ((r >> 3) & 1) * 16 + ((r >> 4) & 3) * 4 + (r >> 6)
        )
        perm_side[...] = one_hot_rows(64, lambda r: (r & 7) * 8 + ((r >> 3) & 1) * 4 + (r >> 4))
        wide = jnp.concatenate(
            [jnp.broadcast_to(wo_ref[c : c + 1, :].astype(F32), (CELLS, C)) for c in range(3)], axis=0
        )
        proj[...] = wide.T.astype(BF)

    for part in range(TH // 4):
        rows = jnp.concatenate(
            [x_ref[g, f * 64 + part * 16 : f * 64 + part * 16 + 16, :] for g in range(GB) for f in range(FC)],
            axis=0,
        )
        moved = dot(perm[...], rows).astype(BF)
        for w in range(TW):
            xt[w, 1 + part * 4 : 5 + part * 4] = moved[w * 64 : w * 64 + 64].reshape(4, GF, C)
    even = even_ref[0]
    for side_ref, row in ((side_a_ref, even * 17), (side_b_ref, (1 - even) * 17)):
        moved = dot(perm_side[...], side_ref[...]).astype(BF)
        for w in range(TW):
            xt[w, pl.ds(row, 1)] = moved[w * 16 : w * 16 + 16].reshape(1, GF, C)

    lane = lax.broadcasted_iota(jnp.int32, (GB, CELLS), 1)
    acc = [jnp.zeros((GB, CELLS), F32) for _ in range(3)]
    t_lhs = jnp.concatenate(
        [
            jnp.concatenate([wt_ref[1], wt_ref[0]], axis=1),
            jnp.concatenate([wt_ref[2], wt_ref[1]], axis=1),
        ],
        axis=0,
    )
    for w in range(TW):
        taps = [(dy, dx) for dx in range(3) if 0 <= w + dx - 1 < TW for dy in range(3)]
        lhs = jnp.concatenate([xt[w + dx - 1, dy : dy + TH].reshape(TH * GF, C) for dy, dx in taps], axis=1)
        rhs = jnp.concatenate([ws_ref[dy, dx] for dy, dx in taps], axis=0)
        act = silu(dot(lhs, rhs)).reshape(TH, FC, GB, C)
        frames = [act[:, f].reshape(TH * GB, C).astype(BF) for f in range(FC)]
        temporal = dot(jnp.concatenate(frames, axis=1), t_lhs)
        field = xt[w, 1 : 1 + TH].astype(F32).reshape(TH, FC, GB, C)
        for f in range(FC):
            mixed = (field[:, f].reshape(TH * GB, C) + temporal[:, f * C : (f + 1) * C]).astype(BF)
            pixels = dot(mixed, proj[...])
            for h in range(TH):
                here = lane == f * TH * TW + h * TW + w
                for c in range(3):
                    acc[c] = jnp.where(here, pixels[h * GB : (h + 1) * GB, c * CELLS : (c + 1) * CELLS], acc[c])
    pix[pl.ds(pl.multiple_of(step * GB, GB), GB), :] = jnp.concatenate(acc, axis=1)

    @pl.when(step == pl.num_programs(0) - 1)
    def _():
        count = owners_ref.shape[0]
        slots = out_ref.shape[0]
        slot = lax.broadcasted_iota(jnp.int32, (count, slots), 1)
        group = lax.broadcasted_iota(jnp.int32, (count, slots), 0)
        named = jnp.broadcast_to(owners_ref[...], (count, slots)) == slot // 2
        earlier = (
            lax.broadcasted_iota(jnp.int32, (count, count), 1) < lax.broadcasted_iota(jnp.int32, (count, count), 0)
        )
        rank = dot(earlier.astype(F32).astype(BF), named.astype(F32).astype(BF))
        placed = named & (rank.astype(jnp.int32) == slot % 2) & (group < live_ref[0])
        out_ref[...] = lax.dot_general(
            placed.astype(F32).astype(BF), pix[...].astype(BF), (((0,), (0,)), ((), ())), preferred_element_type=F32
        ).astype(BF)


def decode(even, live, latents, side_a, side_b, ws, wt, wo, owners):
    groups = latents.shape[0]
    slots = 2 * lax.axis_size("stream")
    whole = lambda shape: pl.BlockSpec(shape, lambda b: (0,) * len(shape))
    return pl.pallas_call(
        decode_kernel,
        grid=(groups // GB,),
        out_shape=jax.ShapeDtypeStruct((slots, 3 * CELLS), BF),
        in_specs=[
            pl.BlockSpec(memory_space=pltpu.SMEM),
            pl.BlockSpec(memory_space=pltpu.SMEM),
            pl.BlockSpec((GB, CELLS, C), lambda b: (b, 0, 0)),
            pl.BlockSpec((GB * FC * TW, C), lambda b: (b, 0)),
            pl.BlockSpec((GB * FC * TW, C), lambda b: (b, 0)),
            whole(ws.shape),
            whole(wt.shape),
            whole(wo.shape),
            whole(owners.shape),
        ],
        out_specs=whole((slots, 3 * CELLS)),
        scratch_shapes=[
            pltpu.VMEM((TW, TH + 2, GF, C), BF),
            pltpu.VMEM((256, 256), BF),
            pltpu.VMEM((64, 64), BF),
            pltpu.VMEM((C, 3 * CELLS), BF),
            pltpu.VMEM((groups, 3 * CELLS), F32),
        ],
        compiler_params=pltpu.CompilerParams(vmem_limit_bytes=32 * 1024 * 1024),
        cost_estimate=pl.CostEstimate(flops=5_000_000_000, bytes_accessed=3_500_000, transcendentals=800_000),
        name="decode",
    )(even, live, latents, side_a, side_b, ws, wt, wo, owners)


def local(latents, owners, live_counts, spatial_weight, temporal_weight, out_weight):
    groups = latents.shape[0]
    latents = latents.reshape(groups, CELLS, C)
    field = latents.reshape(groups, FC, TH, TW, C)
    even = 1 - lax.axis_index("tile") % 2
    head = field[:, :, 0].reshape(groups * FC * TW, C)
    tail = field[:, :, TH - 1].reshape(groups * FC * TW, C)
    send_a = jnp.where(even == 1, tail, head)
    send_b = jnp.where(even == 1, head, tail)
    side_b = lax.ppermute(send_b, "tile", [(1, 2), (2, 1)])
    side_a = lax.ppermute(send_a, "tile", [(0, 1), (1, 0), (2, 3), (3, 2)])
    placed = decode(
        even.reshape(1), live_counts, latents, side_a, side_b, spatial_weight, temporal_weight, out_weight, owners
    )
    streams, bands = lax.axis_size("stream"), lax.axis_size("band")
    outgoing = jnp.broadcast_to(placed.reshape(1, streams, 2, 3 * CELLS), (bands, streams, 2, 3 * CELLS))
    got = lax.all_to_all(
        outgoing.reshape(bands * streams, 2, 3 * CELLS), ("band", "stream"), split_axis=0, concat_axis=0, tiled=True
    )
    parity = lax.axis_index("band")
    signs = 1 - 2 * (lax.population_count(parity & jnp.arange(bands, dtype=jnp.int32)) & 1)
    got = got.reshape(bands, streams * 2, 3, CELLS).astype(F32)
    frames = jnp.sum(got * signs.astype(F32)[:, None, None, None], axis=0) * F32(8.0**-0.5)
    return frames.reshape(streams * 2, 1, 3, CELLS)


def solution(mesh):
    return jax.shard_map(
        local,
        mesh=mesh,
        in_specs=(P("stream", "band", "tile", None), P("stream", None), P("stream"), P(), P(), P()),
        out_specs=P("stream", "band", None, "tile"),
        check_vma=False,
    )
```

time: 101 us -> 69.5 us (0.69); the launches traced: 99.4 us -> 69.3 us
  matrix products: 32.8 us -> 0 us
  blocking collectives: 22.3 us -> 0 us
  Pallas kernels: 0 us -> 12.5 us
  starting transfers between devices: 16.7 us -> 27.5 us
  waiting for transfers between devices: 19.5 us -> 21.2 us
    dot_general x13 -> x0, matrix products: 32.8 us -> none  [the longest x9 18.7 us: decode_items(): jnp.einsum('bfhwc,cd->bfhwd', window, spatial_weight[row_tap, col_tap], p...]
    all_to_all x1 -> x0, blocking collectives: 22.3 us -> none  [local(): lax.all_to_all(outgoing, 'stream', split_axis=0, concat_axis=0, tiled=True)]
    all_to_all x0 -> x1, waiting for transfers between devices: none -> 18.6 us  [local(): lax.all_to_all(outgoing.reshape(bands * streams, 2, 3 * CELLS), ('band',...]
    ppermute x5 -> x2, waiting for transfers between devices: 19.5 us -> 2.61 us  [the longest x1 2.61 us: local(): side_b = lax.ppermute(send_b, 'tile', [(1, 2), (2, 1)])]
    all_to_all x0 -> x1, starting transfers between devices: none -> 16.8 us  [local(): lax.all_to_all(outgoing.reshape(bands * streams, 2, 3 * CELLS), ('band',...]
    pallas_call x0 -> x1, Pallas kernels: none -> 12.5 us  [decode(): pl.pallas_call(decode_kernel, grid=(groups // GB,), out_shape=jax.ShapeDt...]
    ppermute x5 -> x2, starting transfers between devices: 16.7 us -> 10.7 us  [the longest x1 8.77 us: local(): side_a = lax.ppermute(send_a, 'tile', [(0, 1), (1, 0), (2, 3), (3, 2)])]
    unnamed x10 -> x9, local copies, waits for them, and re-layouts: 3.62 us -> 0.75 us
  transfers between devices with their start and end apart: 5 -> 3, of which waited for: 3 -> 2; matrix products, arithmetic and copies ran while one was open for 2% -> 1% of each run, Pallas kernels for 0% -> 0%
where the time goes in v1:
time: 69.5 us; the launch traced here: 69.3 us
  starting transfers between devices  27.5 us (40%)
  waiting for transfers between devices  21.2 us (31%)
  Pallas kernels  12.5 us (18%)
  local copies, waits for them, and re-layouts  6.13 us (9%)
  other arithmetic  1.23 us (2%)
  between operations  0.74 us (1%)
    all_to_all x1, waiting for transfers between devices, local(): lax.all_to_all(outgoing.reshape(bands * streams, 2, 3 * CELLS), ('band',...  18.6 us
    all_to_all x1, starting transfers between devices, local(): lax.all_to_all(outgoing.reshape(bands * streams, 2, 3 * CELLS), ('band',...  16.8 us
    pallas_call x1, Pallas kernels, decode(): pl.pallas_call(decode_kernel, grid=(groups // GB,), out_shape=jax.ShapeDt...  12.5 us
    ppermute x1, starting transfers between devices, local(): side_a = lax.ppermute(send_a, 'tile', [(0, 1), (1, 0), (2, 3), (3, 2)])  8.77 us
    another operation x1, local copies, waits for them, and re-layouts, local(): field = latents.reshape(groups, FC, TH, TW, C)  3.65 us
    ppermute x1, waiting for transfers between devices, local(): side_b = lax.ppermute(send_b, 'tile', [(1, 2), (2, 1)])  2.61 us
    ppermute x1, starting transfers between devices, local(): side_b = lax.ppermute(send_b, 'tile', [(1, 2), (2, 1)])  1.92 us
  transfers between devices with their start and end apart: 3, of which 2 were waited for; matrix products, arithmetic and copies ran while one was open for 1% of the time, Pallas kernels for 0%

profile of v1, /device:TPU:1, one launch (start us, length us, event | category | flops | bytes accessed | tf_op | source)
XLA Modules:
  0.0 69.3 jit_solution(16051231241717661998)
XLA Ops:
  0.0 0.0 copy-start
  0.0 0.0 copy-start.1
  0.0 0.0 copy-start.2
  0.0 0.0 copy-start.3
  0.0 3.7 %reshape_reshape.3 = bf16[24,2,16,4,256]{4,3,2,1,0:T(4,128)(2,1)} reshape(bf16[24,1,128,256]{3,2,1,0:T(8,128)(2,1)} %param.6) | data formatting | bytes 3145728 | tf_op jit(solution)/shard_map/reshape;reshape | solution.py:143
  3.7 1.0 %broadcast_select_fusion = (bf16[24,2,1,4,256]{4,3,1,0,2:T(4,128)(2,1)S(1)}, bf16[24,2,1,4,256]{4,3,1,0,2:T(4,128)(2,1)S(1)}) fusion(pred[]{:T(512)S(6)} %eq.6, bf16[24,2,16,4,256]{4,3,2,1,0:T(4,128)(2,1)} %reshape_reshape.3), kind=kLoop, calls=%fused_computation.3 | loop fusion | flops 98304 | bytes 393217 | tf_op jit(solution)/shard_map/jit(_where)/select_n | solution.py:148
  4.7 8.8 %collective-permute-start = (bf16[192,256]{1,0:T(8,128)(2,1)S(1)}, bf16[192,256]{1,0:T(8,128)(2,1)S(1)}, u32[]{:S(2)}, u32[]{:S(2)}) collective-permute-start(bf16[192,256]{1,0:T(8,128)(2,1)S(1)} %select_n.28), channel_id=1, source_target_pairs={{0,8},{8,0},{16,24},{24,16},{1,9},{9,1},{17,25},{25,17},{2,10},{10... | collective-permute-start | bytes 294920 | tf_op jit(solution)/shard_map/ppermute | solution.py:150
  13.6 1.9 %collective-permute-start.1 = (bf16[192,256]{1,0:T(8,128)(2,1)S(1)}, bf16[192,256]{1,0:T(8,128)(2,1)S(1)}, u32[]{:S(2)}, u32[]{:S(2)}) collective-permute-start(bf16[192,256]{1,0:T(8,128)(2,1)S(1)} %select_n.30), channel_id=1, source_target_pairs={{8,16},{16,8},{9,17},{17,9},{10,18},{18,10},{11,19},{19,11},{12,20... | collective-permute-start | bytes 294920 | tf_op jit(solution)/shard_map/ppermute | solution.py:149
  15.5 0.7 %copy.21.owners_ref = s32[24,1]{1,0:T(8,128)S(1)} copy(s32[24,1]{0,1:T(1,128)} %param.7) | data formatting | bytes 192 | tf_op args[1]
  16.9 0.0 collective-permute-done.side_a_ref
  16.9 2.6 %collective-permute-done.1.side_b_ref = bf16[192,256]{1,0:T(8,128)(2,1)S(1)} collective-permute-done((bf16[192,256]{1,0:T(8,128)(2,1)S(1)}, bf16[192,256]{1,0:T(8,128)(2,1)S(1)}, u32[]{:S(2)}, u32[]{:S(2)}) %collective-permute-start.1) | collective-permute-done | bytes 98336 | tf_op jit(solution)/shard_map/ppermute | solution.py:149
  19.5 0.0 copy-done
  19.5 0.0 copy-done.1
  19.5 0.0 copy-done.2
  19.5 0.0 copy-done.3
  19.5 12.5 %decode.1 = bf16[32,384]{1,0:T(8,128)(2,1)S(1)} custom-call(s32[1]{0:T(128)} %bitcast.even_ref, s32[1]{0:T(128)S(6)} %copy.29.live_ref, bf16[24,128,256]{2,1,0:T(8,128)(2,1)S(1)} %bitcast.23, bf16[192,256]{1,0:T(8,128)(2,1)S(1)} %collective-permute-done.side_a_ref, bf16[192,256]{1,0:T(8,128)(2,1)S(1)} %collective-permute-done.1.side_b_ref, ...), custom_call_target="tpu_custom_call" | custom-call | flops 5000000000 | bytes 3500000 | tf_op jit(solution)/shard_map/decode/pallas_call | solution.py:111
  32.1 0.8 %broadcast_in_dim.9 = bf16[8,16,2,384]{3,2,1,0:T(2,128)(2,1)} broadcast(bf16[16,2,384]{2,1,0:T(2,128)(2,1)S(1)} %broadcast_in_dim.8), dimensions={1,2,3} | broadcast | bytes 221184 | tf_op jit(solution)/shard_map/broadcast_in_dim | solution.py:155
  32.8 16.8 %all-to-all-start = ((bf16[128,2,384]{2,1,0:T(2,128)(2,1)}), bf16[128,2,384]{2,1,0:T(2,128)(2,1)S(1)}, u32[]{:S(2)}, u32[]{:S(2)}) async-start(bf16[128,2,384]{2,1,0:T(2,128)(2,1)} %bitcast.2), calls=%async_computation | async-start | bytes 393216 | tf_op jit(solution)/shard_map/all_to_all | solution.py:156
  49.6 18.6 %all-to-all-done = bf16[128,2,384]{2,1,0:T(2,128)(2,1)S(1)} async-done(((bf16[128,2,384]{2,1,0:T(2,128)(2,1)}), bf16[128,2,384]{2,1,0:T(2,128)(2,1)S(1)}, u32[]{:S(2)}, u32[]{:S(2)}) %all-to-all-start) | async-done | bytes 196640 | tf_op jit(solution)/shard_map/all_to_all | solution.py:156
  68.2 0.2 reshape.40
  68.4 0.2 multiply_reduce_fusion
  68.6 0.7 copy.23
  (5 shorter events, 0.1 us)
Async XLA Ops:
  0.0 19.5 %copy-start = (bf16[24,1,128,256]{3,2,1,0:T(8,128)(2,1)S(1)}, bf16[24,1,128,256]{3,2,1,0:T(8,128)(2,1)}, u32[]{:S(2)}) copy-start(bf16[24,1,128,256]{3,2,1,0:T(8,128)(2,1)} %param.6) | copy-start | bytes 4718596
  0.0 19.5 %copy-start.1 = (bf16[3,3,256,256]{3,2,1,0:T(8,128)(2,1)S(1)}, bf16[3,3,256,256]{3,2,1,0:T(8,128)(2,1)}, u32[]{:S(2)}) copy-start(bf16[3,3,256,256]{3,2,1,0:T(8,128)(2,1)} %ws_ref.1) | copy-start | bytes 3538948
  0.0 19.5 %copy-start.2 = (bf16[3,256,256]{2,1,0:T(8,128)(2,1)S(1)}, bf16[3,256,256]{2,1,0:T(8,128)(2,1)}, u32[]{:S(2)}) copy-start(bf16[3,256,256]{2,1,0:T(8,128)(2,1)} %wt_ref.1) | copy-start | bytes 1179652
  0.0 19.5 %copy-start.3 = (bf16[3,256]{1,0:T(4,128)(2,1)S(1)}, bf16[3,256]{1,0:T(4,128)(2,1)}, u32[]{:S(2)}) copy-start(bf16[3,256]{1,0:T(4,128)(2,1)} %wo_ref.1) | copy-start | bytes 4612
  4.7 12.1 %collective-permute-start = (bf16[192,256]{1,0:T(8,128)(2,1)S(1)}, bf16[192,256]{1,0:T(8,128)(2,1)S(1)}, u32[]{:S(2)}, u32[]{:S(2)}) collective-permute-start(bf16[192,256]{1,0:T(8,128)(2,1)S(1)} %select_n.28), channel_id=1, source_target_pairs={{0,8},{8,0},{16,24},{24,16},{1,9},{9,1},{17,25},{25,17},{2,10},{10... | collective-permute-start | bytes 294920 | tf_op jit(solution)/shard_map/ppermute | solution.py:150
  13.6 5.9 %collective-permute-start.1 = (bf16[192,256]{1,0:T(8,128)(2,1)S(1)}, bf16[192,256]{1,0:T(8,128)(2,1)S(1)}, u32[]{:S(2)}, u32[]{:S(2)}) collective-permute-start(bf16[192,256]{1,0:T(8,128)(2,1)S(1)} %select_n.30), channel_id=1, source_target_pairs={{8,16},{16,8},{9,17},{17,9},{10,18},{18,10},{11,19},{19,11},{12,20... | collective-permute-start | bytes 294920 | tf_op jit(solution)/shard_map/ppermute | solution.py:149
  32.8 35.4 %all-to-all-start = ((bf16[128,2,384]{2,1,0:T(2,128)(2,1)}), bf16[128,2,384]{2,1,0:T(2,128)(2,1)S(1)}, u32[]{:S(2)}, u32[]{:S(2)}) async-start(bf16[128,2,384]{2,1,0:T(2,128)(2,1)} %bitcast.2), calls=%async_computation | async-start | bytes 393216 | tf_op jit(solution)/shard_map/all_to_all | solution.py:156

commit v2 on v1

v2 whole, which is shorter than its diff:
```python
import jax
import jax.numpy as jnp
from jax import lax
from jax.experimental import pallas as pl
from jax.experimental.pallas import tpu as pltpu
from jax.sharding import PartitionSpec as P

C = 256
FC = 2
TH = 16
TW = 4
GB = 8
GF = FC * GB
CELLS = FC * TH * TW
HALF = TH * TW
BF = jnp.bfloat16
F32 = jnp.float32


def dot(a, b):
    return lax.dot_general(a, b, (((1,), (0,)), ((), ())), preferred_element_type=F32)


def silu(x):
    return 0.5 * x * (1.0 + jnp.tanh(0.5 * x))


def one_hot(rows, cols, place):
    row = lax.broadcasted_iota(jnp.int32, (rows, cols), 0)
    col = lax.broadcasted_iota(jnp.int32, (rows, cols), 1)
    return (place(row) == col).astype(F32).astype(BF)


def temporal_matrix(wt_ref):
    first = jnp.concatenate([wt_ref[1], wt_ref[0]], axis=1)
    second = jnp.concatenate([wt_ref[2], wt_ref[1]], axis=1)
    return jnp.concatenate([first, second], axis=0)


def edges_kernel(even_ref, x_ref, a_ref, b_ref, slab, sems):
    even = even_ref[0]
    blocks = x_ref.shape[0] // GB
    copies = []
    for side in range(2):
        last = even if side == 0 else 1 - even
        for f in range(FC):
            start = pl.multiple_of(f * HALF + last * (HALF - 8), 8)
            copies.append(
                pltpu.make_async_copy(x_ref.at[:, pl.ds(start, 8), :], slab.at[side, f], sems.at[side, f])
            )
    for copy in copies:
        copy.start()
    for side, out_ref in enumerate((a_ref, b_ref)):
        last = even if side == 0 else 1 - even
        pick = one_hot(
            TW * GF, FC * GB * 8, lambda r: ((r >> 3) & 1) * (GB * 8) + (r & 7) * 8 + last * 4 + (r >> 4)
        )
        for f in range(FC):
            copies[side * FC + f].wait()
        for b in range(blocks):
            rows = slab[side, :, b * GB : (b + 1) * GB].reshape(FC * GB * 8, C)
            moved = dot(pick, rows).astype(BF)
            for w in range(TW):
                at = (w * blocks + b) * GF
                out_ref[at : at + GF, :] = moved[w * GF : (w + 1) * GF]


def edges(even, latents):
    groups = latents.shape[0]
    side = jax.ShapeDtypeStruct((TW * groups * FC, C), BF)
    vmem = pl.BlockSpec(memory_space=pltpu.VMEM)
    return pl.pallas_call(
        edges_kernel,
        out_shape=(side, side),
        in_specs=[pl.BlockSpec(memory_space=pltpu.SMEM), pl.BlockSpec(memory_space=pltpu.HBM)],
        out_specs=(vmem, vmem),
        scratch_shapes=[pltpu.VMEM((2, FC, groups, 8, C), BF), pltpu.SemaphoreType.DMA((2, FC))],
        cost_estimate=pl.CostEstimate(flops=50_000_000, bytes_accessed=800_000, transcendentals=0),
        name="edges",
    )(even, latents)


def main_kernel(x_ref, ws_ref, wt_ref, wo_ref, rim_ref, field_ref, sums_ref, proj_ref, xt, act, mix):
    blocks = x_ref.shape[0] // GB
    width = blocks * GF
    half = blocks * GB
    perm = one_hot(256, 256, lambda r: (r & 7) * 32 + ((r >> 3) & 1) * 16 + ((r >> 4) & 3) * 4 + (r >> 6))
    wide = [jnp.broadcast_to(wo_ref[min(c, 2) : min(c, 2) + 1, :].astype(F32), (HALF, C)) for c in range(4)]
    proj_ref[...] = jnp.concatenate(wide, axis=0).T.astype(BF)
    zero_row = jnp.zeros((width, C), BF)
    for w in range(TW):
        xt[w, 0] = zero_row
        xt[w, TH + 1] = zero_row
    for b in range(blocks):
        for part in range(TH // 4):
            rows = jnp.concatenate(
                [
                    x_ref[b * GB + g, f * HALF + part * 16 : f * HALF + part * 16 + 16, :]
                    for g in range(GB)
                    for f in range(FC)
                ],
                axis=0,
            )
            moved = dot(perm, rows).astype(BF)
            for w in range(TW):
                xt[w, 1 + part * 4 : 5 + part * 4, b * GF : (b + 1) * GF] = moved[w * 64 : w * 64 + 64].reshape(4, GF, C)
    inner = TH - 2
    for w in range(TW):
        taps = [(dy, dx) for dx in range(3) if 0 <= w + dx - 1 < TW for dy in range(3)]
        lhs = jnp.concatenate([xt[w + dx - 1, dy : dy + TH].reshape(TH * width, C) for dy, dx in taps], axis=1)
        rhs = jnp.concatenate([ws_ref[dy, dx] for dy, dx in taps], axis=0)
        total = dot(lhs, rhs).reshape(TH, width, C)
        rim_ref[0, w] = total[0]
        rim_ref[1, w] = total[TH - 1]
        field_ref[0, w] = xt[w, 1]
        field_ref[1, w] = xt[w, TH]
        live = silu(total[1 : TH - 1].reshape(inner * width, C)).reshape(inner * blocks, FC, GB, C)
        for f in range(FC):
            act[w, :, f * C : (f + 1) * C] = live[:, f].reshape(inner * half, C).astype(BF)
    for w in range(TW):
        temporal = dot(act[w], temporal_matrix(wt_ref))
        field = xt[w, 2:TH].astype(F32).reshape(inner * blocks, FC, GB, C)
        for f in range(FC):
            mix[w, f] = (field[:, f].reshape(inner * half, C) + temporal[:, f * C : (f + 1) * C]).astype(BF)
    lane = lax.broadcasted_iota(jnp.int32, (GB, 4 * HALF), 1) & (HALF - 1)
    sums = [[jnp.zeros((GB, 4 * HALF), F32) for _ in range(FC)] for _ in range(blocks)]
    for w in range(TW):
        for f in range(FC):
            pixels = dot(mix[w, f], proj_ref[...])
            for h in range(inner):
                here = lane == (h + 1) * TW + w
                for b in range(blocks):
                    at = (h * blocks + b) * GB
                    sums[b][f] = jnp.where(here, pixels[at : at + GB], sums[b][f])
    for b in range(blocks):
        for f in range(FC):
            sums_ref[b, f] = sums[b][f]


def main(latents, ws, wt, wo):
    groups = latents.shape[0]
    width = groups * FC
    vmem = pl.BlockSpec(memory_space=pltpu.VMEM)
    return pl.pallas_call(
        main_kernel,
        out_shape=(
            jax.ShapeDtypeStruct((2, TW, width, C), F32),
            jax.ShapeDtypeStruct((2, TW, width, C), BF),
            jax.ShapeDtypeStruct((groups // GB, FC, GB, 4 * HALF), F32),
            jax.ShapeDtypeStruct((C, 4 * HALF), BF),
        ),
        in_specs=[vmem] * 4,
        out_specs=(vmem,) * 4,
        scratch_shapes=[
            pltpu.VMEM((TW, TH + 2, width, C), BF),
            pltpu.VMEM((TW, (TH - 2) * groups, FC * C), BF),
            pltpu.VMEM((TW, FC, (TH - 2) * groups, C), BF),
        ],
        compiler_params=pltpu.CompilerParams(vmem_limit_bytes=32 * 1024 * 1024),
        cost_estimate=pl.CostEstimate(flops=5_000_000_000, bytes_accessed=4_500_000, transcendentals=700_000),
        name="main",
    )(latents, ws, wt, wo)


def finish_kernel(
    even_ref, live_ref, a_ref, b_ref, rim_ref, field_ref, sums_ref, proj_ref, ws_ref, wt_ref, owners_ref, out_ref
):
    blocks = sums_ref.shape[0]
    count = blocks * GB
    width = count * FC
    even = even_ref[0] == 1
    top = jnp.where(even, b_ref[...], a_ref[...])
    bottom = jnp.where(even, a_ref[...], b_ref[...])
    acts = []
    for side, (halo, dy) in enumerate(((top, 0), (bottom, 2))):
        total = rim_ref[side].reshape(TW * width, C) + dot(halo, ws_ref[dy, 1])
        left = dot(halo[: (TW - 1) * width], ws_ref[dy, 0])
        right = dot(halo[width:], ws_ref[dy, 2])
        gap = jnp.zeros((width, C), F32)
        total = total + jnp.concatenate([gap, left], axis=0) + jnp.concatenate([right, gap], axis=0)
        acts.append(silu(total).reshape(TW * blocks, FC, GB, C))
    frames = [
        jnp.concatenate([acts[side][:, f].reshape(TW * count, C) for side in range(2)], axis=0).astype(BF)
        for f in range(FC)
    ]
    temporal = dot(jnp.concatenate(frames, axis=1), temporal_matrix(wt_ref))
    field = field_ref[...].astype(F32).reshape(2 * TW * blocks, FC, GB, C)
    lane = lax.broadcasted_iota(jnp.int32, (GB, 4 * HALF), 1) & (HALF - 1)
    narrow = lax.broadcasted_iota(jnp.int32, (GB, CELLS), 1) < HALF
    sums = [[sums_ref[b, f] for f in range(FC)] for b in range(blocks)]
    for f in range(FC):
        mixed = (field[:, f].reshape(2 * TW * count, C) + temporal[:, f * C : (f + 1) * C]).astype(BF)
        pixels = dot(mixed, proj_ref[...])
        for side, h in ((0, 0), (1, TH - 1)):
            for w in range(TW):
                here = lane == h * TW + w
                for b in range(blocks):
                    at = ((side * TW + w) * blocks + b) * GB
                    sums[b][f] = jnp.where(here, pixels[at : at + GB], sums[b][f])
    channels = []
    for c in range(3):
        at = c // 2 * CELLS
        for b in range(blocks):
            first, second = sums[b][0][:, at : at + CELLS], sums[b][1][:, at : at + CELLS]
            if c % 2 == 0:
                second = pltpu.roll(second, HALF, 1)
            else:
                first = pltpu.roll(first, HALF, 1)
            channels.append(jnp.where(narrow, first, second))
    stacked = jnp.concatenate(channels, axis=0).astype(BF)
    slots = out_ref.shape[0] // 8
    row = lax.broadcasted_iota(jnp.int32, (slots, count), 0) // 3
    group = lax.broadcasted_iota(jnp.int32, (slots, count), 1)
    named = jnp.broadcast_to(owners_ref[...], (slots, count)) == row // 2
    earlier = lax.broadcasted_iota(jnp.int32, (count, count), 0) < lax.broadcasted_iota(jnp.int32, (count, count), 1)
    rank = dot(named.astype(F32).astype(BF), earlier.astype(F32).astype(BF)).astype(jnp.int32)
    placed = named & (rank == row % 2) & (group < live_ref[0])
    channel = lax.broadcasted_iota(jnp.int32, (slots, count), 0) % 3
    placing = jnp.concatenate([(placed & (channel == c)).astype(F32) for c in range(3)], axis=1).astype(BF)
    message = dot(placing, stacked).astype(BF)
    for p in range(8):
        out_ref[p * slots : (p + 1) * slots, :] = message


def finish(even, live, side_a, side_b, rim, field, sums, proj, ws, wt, owners, rows):
    vmem = pl.BlockSpec(memory_space=pltpu.VMEM)
    smem = pl.BlockSpec(memory_space=pltpu.SMEM)
    return pl.pallas_call(
        finish_kernel,
        out_shape=jax.ShapeDtypeStruct((rows, CELLS), BF),
        in_specs=[smem, smem] + [vmem] * 9,
        out_specs=vmem,
        compiler_params=pltpu.CompilerParams(vmem_limit_bytes=32 * 1024 * 1024),
        cost_estimate=pl.CostEstimate(flops=500_000_000, bytes_accessed=3_000_000, transcendentals=100_000),
        name="finish",
    )(even, live, side_a, side_b, rim, field, sums, proj, ws, wt, owners)


def local(latents, owners, live_counts, spatial_weight, temporal_weight, out_weight):
    groups = latents.shape[0]
    latents = latents.reshape(groups, CELLS, C)
    streams, bands = lax.axis_size("stream"), lax.axis_size("band")
    even = (1 - (lax.axis_index("tile") & 1)).reshape(1)
    send_a, send_b = edges(even, latents)
    side_b = lax.ppermute(send_b, "tile", [(1, 2), (2, 1)])
    side_a = lax.ppermute(send_a, "tile", [(0, 1), (1, 0), (2, 3), (3, 2)])
    rim, field, sums, proj = main(latents, spatial_weight, temporal_weight, out_weight)
    rows = bands * streams * 2 * 3
    outgoing = finish(
        even, live_counts, side_a, side_b, rim, field, sums, proj, spatial_weight, temporal_weight,
        owners.reshape(1, groups), rows,
    )
    parity = lax.axis_index("band")
    signs = 1 - 2 * (lax.population_count(parity & jnp.arange(bands, dtype=jnp.int32)) & 1)
    signs = signs.astype(F32) * F32(8.0**-0.5)
    outgoing, signs = lax.optimization_barrier((outgoing.reshape(rows // 2, 2, CELLS), signs))
    got = lax.all_to_all(outgoing, ("band", "stream"), split_axis=0, concat_axis=0, tiled=True)
    got = got.reshape(bands, streams * 2 * 3, CELLS).astype(F32)
    frames = jnp.sum(got * signs[:, None, None], axis=0)
    return frames.reshape(streams * 2, 1, 3, CELLS)


def solution(mesh):
    return jax.shard_map(
        local,
        mesh=mesh,
        in_specs=(P("stream", "band", "tile", None), P("stream", None), P("stream"), P(), P(), P()),
        out_specs=P("stream", "band", None, "tile"),
        check_vma=False,
    )
```

time: 69.5 us -> 60 us (0.86)
  blocking collectives: 0 us -> 37.5 us
  waiting for transfers between devices: 21.2 us -> 0.01 us
  starting transfers between devices: 27.5 us -> 10.7 us
  Pallas kernels: 12.5 us -> 7.72 us
  local copies, waits for them, and re-layouts: 6.13 us -> 2.28 us
    all_to_all x0 -> x1, blocking collectives: none -> 37.5 us  [local(): lax.all_to_all(outgoing, ('band', 'stream'), split_axis=0, concat_axis=0,...]
    all_to_all x1 -> x0, waiting for transfers between devices: 18.6 us -> none  [local(): lax.all_to_all(outgoing.reshape(bands * streams, 2, 3 * CELLS), ('band',...]
    all_to_all x1 -> x0, starting transfers between devices: 16.8 us -> none  [local(): lax.all_to_all(outgoing.reshape(bands * streams, 2, 3 * CELLS), ('band',...]
    pallas_call x1 -> x3, Pallas kernels: 12.5 us -> 7.72 us  [the longest x1 4.75 us: main(): pl.pallas_call(main_kernel, out_shape=(jax.ShapeDtypeStruct((2, TW, width...]
    another operation x1 -> x0, local copies, waits for them, and re-layouts: 3.65 us -> none  [local(): field = latents.reshape(groups, FC, TH, TW, C)]
    ppermute x1, waiting for transfers between devices: 2.61 us -> 0.01 us  [local(): side_b = lax.ppermute(send_b, 'tile', [(1, 2), (2, 1)])]
    unnamed x9 -> x12, local copies, waits for them, and re-layouts: 0.75 us -> 2.28 us
    select_n x1 -> x0, other arithmetic: 1.03 us -> none  [local(): send_b = jnp.where(even == 1, head, tail)]
  transfers between devices with their start and end apart: 3 -> 2, of which waited for: 2 -> 0; matrix products, arithmetic and copies ran while one was open for 1% -> 0% of each run, Pallas kernels for 0% -> 8%
where the time goes in v2:
time: 60 us; the launch traced here: 59.7 us
  blocking collectives  37.5 us (62%)
  starting transfers between devices  10.7 us (18%)
  Pallas kernels  7.72 us (13%)
  local copies, waits for them, and re-layouts  2.28 us (4%)
  between operations  0.75 us (1%)
  other arithmetic  0.74 us (1%)
    all_to_all x1, blocking collectives, local(): lax.all_to_all(outgoing, ('band', 'stream'), split_axis=0, concat_axis=0,...  37.5 us
    ppermute x1, starting transfers between devices, local(): side_a = lax.ppermute(send_a, 'tile', [(0, 1), (1, 0), (2, 3), (3, 2)])  8.78 us
    pallas_call x1, Pallas kernels, main(): pl.pallas_call(main_kernel, out_shape=(jax.ShapeDtypeStruct((2, TW, width...  4.75 us
    unnamed x12, local copies, waits for them, and re-layouts  2.28 us
    pallas_call x1, Pallas kernels, edges(): pl.pallas_call(edges_kernel, out_shape=(side, side), in_specs=[pl.BlockSp...  2.07 us
    ppermute x1, starting transfers between devices, local(): side_b = lax.ppermute(send_b, 'tile', [(1, 2), (2, 1)])  1.92 us
  transfers between devices with their start and end apart: 2, of which 0 were waited for; matrix products, arithmetic and copies ran while one was open for 0% of the time, Pallas kernels for 8%

profile of v2, /device:TPU:1, one launch (start us, length us, event | category | flops | bytes accessed | tf_op | source)
XLA Modules:
  0.0 59.7 jit_solution(16597906317471882476)
XLA Ops:
  0.0 0.0 copy-start
  0.0 0.0 copy-start.5
  0.0 2.1 %edges.1 = (bf16[192,256]{1,0:T(8,128)(2,1)}, bf16[192,256]{1,0:T(8,128)(2,1)}) custom-call(s32[1]{0:T(128)} %bitcast.even_ref, bf16[24,128,256]{2,1,0:T(8,128)(2,1)} %bitcast.9), custom_call_target="tpu_custom_call" | custom-call | flops 50000000 | bytes 800000 | tf_op jit(solution)/shard_map/edges/pallas_call | solution.py:72
  2.1 8.8 %collective-permute-start = (bf16[192,256]{1,0:T(8,128)(2,1)}, bf16[192,256]{1,0:T(8,128)(2,1)S(1)}, u32[]{:S(2)}, u32[]{:S(2)}) collective-permute-start(bf16[192,256]{1,0:T(8,128)(2,1)} %get-tuple-element.13), channel_id=1, source_target_pairs={{0,8},{8,0},{16,24},{24,16},{1,9},{9,1},{17,25},{25,17},{2,10},{10... | collective-permute-start | bytes 294920 | tf_op jit(solution)/shard_map/ppermute | solution.py:246
  10.9 1.9 %collective-permute-start.1 = (bf16[192,256]{1,0:T(8,128)(2,1)}, bf16[192,256]{1,0:T(8,128)(2,1)S(1)}, u32[]{:S(2)}, u32[]{:S(2)}) collective-permute-start(bf16[192,256]{1,0:T(8,128)(2,1)} %get-tuple-element.14), channel_id=1, source_target_pairs={{8,16},{16,8},{9,17},{17,9},{10,18},{18,10},{11,19},{19,11},{12,20... | collective-permute-start | bytes 294920 | tf_op jit(solution)/shard_map/ppermute | solution.py:245
  13.5 0.0 copy-done
  13.5 0.0 copy-done.5
  13.5 0.0 copy-start.1
  13.5 1.3 %copy-done.1 = bf16[3,3,256,256]{3,2,1,0:T(8,128)(2,1)S(1)} copy-done((bf16[3,3,256,256]{3,2,1,0:T(8,128)(2,1)S(1)}, bf16[3,3,256,256]{3,2,1,0:T(8,128)(2,1)}, u32[]{:S(2)}) %copy-start.1) | copy-done | bytes 1179672
  14.7 0.0 copy-start.3
  14.7 1.0 %copy-done.3 = bf16[3,256,256]{2,1,0:T(8,128)(2,1)S(1)} copy-done((bf16[3,256,256]{2,1,0:T(8,128)(2,1)S(1)}, bf16[3,256,256]{2,1,0:T(8,128)(2,1)}, u32[]{:S(2)}) %copy-start.3) | copy-done | bytes 393240
  15.7 0.0 copy-start.2
  15.7 0.0 copy-start.4
  15.7 4.8 %main.1 = (f32[2,4,48,256]{3,2,1,0:T(8,128)S(1)}, bf16[2,4,48,256]{3,2,1,0:T(8,128)(2,1)S(1)}, f32[3,2,8,256]{3,2,1,0:T(8,128)S(1)}, bf16[256,256]{1,0:T(8,128)(2,1)S(1)}) custom-call(bf16[24,128,256]{2,1,0:T(8,128)(2,1)S(1)} %bitcast.10, bf16[3,3,256,256]{3,2,1,0:T(8,128)(2,1)S(1)} %copy-done.1, bf16[3,256,256]{2,1,0:T(8,128)(2,1)S(1)} %copy-done.3, ...), custom_call_target="tpu_custom_call" | custom-call | flops 5000000000 | bytes 4500000 | tf_op jit(solution)/shard_map/main/pallas_call | solution.py:144
  20.5 0.0 collective-permute-done.a_ref
  20.5 0.0 collective-permute-done.1.b_ref
  20.5 0.0 copy-done.2
  20.6 0.0 copy-done.4
  20.6 0.9 %finish.1 = bf16[768,128]{1,0:T(8,128)(2,1)S(1)} custom-call(s32[1]{0:T(128)} %bitcast.even_ref, s32[1]{0:T(128)S(6)} %copy.7.live_ref, bf16[192,256]{1,0:T(8,128)(2,1)S(1)} %collective-permute-done.a_ref, bf16[192,256]{1,0:T(8,128)(2,1)S(1)} %collective-permute-done.1.b_ref, f32[2,4,48,256]{3,2,1,0:T(8,128)S(1)} %get-tuple-element.15.rim_ref, ...), custom_call_target="tpu_custom_call" | custom-call | flops 500000000 | bytes 3000000 | tf_op jit(solution)/shard_map/finish/pallas_call | solution.py:228
  21.5 37.5 %all_to_all.5 = bf16[384,2,128]{2,1,0:T(2,128)(2,1)S(1)} all-to-all(bf16[384,2,128]{2,1,0:T(2,128)(2,1)S(1)} %bitcast.11), channel_id=1, replica_groups=mesh['stream'=16,'tile'=4,'band'=8] {'band','stream'}, dimensions={0} | all-to-all | bytes 393216 | tf_op jit(solution)/shard_map/all_to_all | solution.py:257
  59.0 0.7 %fusion = f32[96,128]{1,0:T(8,128)} fusion(f32[8]{0:T(128)S(1)} %convert_multiply_fusion.1, bf16[8,96,128]{2,1,0:T(8,128)(2,1)S(1)} %bitcast.13), kind=kLoop, calls=%fused_computation.1 | loop fusion | flops 282624 | bytes 245792 | tf_op jit(solution)/shard_map/reduce_sum | solution.py:259
  (1 shorter events, 0.0 us)
Async XLA Ops:
  0.0 13.5 %copy-start = (bf16[24,1,128,256]{3,2,1,0:T(8,128)(2,1)S(1)}, bf16[24,1,128,256]{3,2,1,0:T(8,128)(2,1)}, u32[]{:S(2)}) copy-start(bf16[24,1,128,256]{3,2,1,0:T(8,128)(2,1)} %param.6) | copy-start | bytes 4718596
  0.0 13.5 %copy-start.5 = (bf16[3,256]{1,0:T(4,128)(2,1)S(1)}, bf16[3,256]{1,0:T(4,128)(2,1)}, u32[]{:S(2)}) copy-start(bf16[3,256]{1,0:T(4,128)(2,1)} %wo_ref.1) | copy-start | bytes 4612
  2.1 18.4 %collective-permute-start = (bf16[192,256]{1,0:T(8,128)(2,1)}, bf16[192,256]{1,0:T(8,128)(2,1)S(1)}, u32[]{:S(2)}, u32[]{:S(2)}) collective-permute-start(bf16[192,256]{1,0:T(8,128)(2,1)} %get-tuple-element.13), channel_id=1, source_target_pairs={{0,8},{8,0},{16,24},{24,16},{1,9},{9,1},{17,25},{25,17},{2,10},{10... | collective-permute-start | bytes 294920 | tf_op jit(solution)/shard_map/ppermute | solution.py:246
  10.9 9.7 %collective-permute-start.1 = (bf16[192,256]{1,0:T(8,128)(2,1)}, bf16[192,256]{1,0:T(8,128)(2,1)S(1)}, u32[]{:S(2)}, u32[]{:S(2)}) collective-permute-start(bf16[192,256]{1,0:T(8,128)(2,1)} %get-tuple-element.14), channel_id=1, source_target_pairs={{8,16},{16,8},{9,17},{17,9},{10,18},{18,10},{11,19},{19,11},{12,20... | collective-permute-start | bytes 294920 | tf_op jit(solution)/shard_map/ppermute | solution.py:245
  13.5 1.3 %copy-start.1 = (bf16[3,3,256,256]{3,2,1,0:T(8,128)(2,1)S(1)}, bf16[3,3,256,256]{3,2,1,0:T(8,128)(2,1)}, u32[]{:S(2)}) copy-start(bf16[3,3,256,256]{3,2,1,0:T(8,128)(2,1)} %ws_ref.3) | copy-start | bytes 3538948
  14.7 1.0 %copy-start.3 = (bf16[3,256,256]{2,1,0:T(8,128)(2,1)S(1)}, bf16[3,256,256]{2,1,0:T(8,128)(2,1)}, u32[]{:S(2)}) copy-start(bf16[3,256,256]{2,1,0:T(8,128)(2,1)} %wt_ref.3) | copy-start | bytes 1179652
  15.7 4.8 %copy-start.2 = (bf16[3,3,256,256]{3,2,1,0:T(8,128)(2,1)S(1)}, bf16[3,3,256,256]{3,2,1,0:T(8,128)(2,1)}, u32[]{:S(2)}) copy-start(bf16[3,3,256,256]{3,2,1,0:T(8,128)(2,1)} %ws_ref.3) | copy-start | bytes 3538948
  15.7 4.8 %copy-start.4 = (s32[24,1]{0,1:T(1,128)S(1)}, s32[24,1]{0,1:T(1,128)}, u32[]{:S(2)}) copy-start(s32[24,1]{0,1:T(1,128)} %param.7) | copy-start | bytes 292

commit v3 on v2

--- a/solution.py
+++ b/solution.py
@@ -37,65 +37,34 @@
     return jnp.concatenate([first, second], axis=0)
 
 
-def edges_kernel(even_ref, x_ref, a_ref, b_ref, slab, sems):
-    even = even_ref[0]
-    blocks = x_ref.shape[0] // GB
-    copies = []
-    for side in range(2):
-        last = even if side == 0 else 1 - even
-        for f in range(FC):
-            start = pl.multiple_of(f * HALF + last * (HALF - 8), 8)
-            copies.append(
-                pltpu.make_async_copy(x_ref.at[:, pl.ds(start, 8), :], slab.at[side, f], sems.at[side, f])
-            )
-    for copy in copies:
+def prep_kernel(
+    even_ref, x_ref, ws_ref, wo_ref, a_ref, b_ref, xt_ref, ws_out, proj_ref, slab, wo_buf, sems
+):
+    groups = x_ref.shape[0]
+    blocks = groups // GB
+    width = blocks * GF
+    x_copies = [
+        pltpu.make_async_copy(x_ref.at[b * GB : (b + 1) * GB], slab.at[b * GB : (b + 1) * GB], sems.at[b])
+        for b in range(blocks)
+    ]
+    wo_copy = pltpu.make_async_copy(wo_ref, wo_buf, sems.at[blocks])
+    ws_copy = pltpu.make_async_copy(ws_ref, ws_out, sems.at[blocks + 1])
+    for copy in [wo_copy] + x_copies + [ws_copy]:
         copy.start()
-    for side, out_ref in enumerate((a_ref, b_ref)):
-        last = even if side == 0 else 1 - even
-        pick = one_hot(
-            TW * GF, FC * GB * 8, lambda r: ((r >> 3) & 1) * (GB * 8) + (r & 7) * 8 + last * 4 + (r >> 4)
-        )
-        for f in range(FC):
-            copies[side * FC + f].wait()
-        for b in range(blocks):
-            rows = slab[side, :, b * GB : (b + 1) * GB].reshape(FC * GB * 8, C)
-            moved = dot(pick, rows).astype(BF)
-            for w in range(TW):
-                at = (w * blocks + b) * GF
-                out_ref[at : at + GF, :] = moved[w * GF : (w + 1) * GF]
-
-
-def edges(even, latents):
-    groups = latents.shape[0]
-    side = jax.ShapeDtypeStruct((TW * groups * FC, C), BF)
-    vmem = pl.BlockSpec(memory_space=pltpu.VMEM)
-    return pl.pallas_call(
-        edges_kernel,
-        out_shape=(side, side),
-        in_specs=[pl.BlockSpec(memory_space=pltpu.SMEM), pl.BlockSpec(memory_space=pltpu.HBM)],
-        out_specs=(vmem, vmem),
-        scratch_shapes=[pltpu.VMEM((2, FC, groups, 8, C), BF), pltpu.SemaphoreType.DMA((2, FC))],
-        cost_estimate=pl.CostEstimate(flops=50_000_000, bytes_accessed=800_000, transcendentals=0),
-        name="edges",
-    )(even, latents)
-
-
-def main_kernel(x_ref, ws_ref, wt_ref, wo_ref, rim_ref, field_ref, sums_ref, proj_ref, xt, act, mix):
-    blocks = x_ref.shape[0] // GB
-    width = blocks * GF
-    half = blocks * GB
     perm = one_hot(256, 256, lambda r: (r & 7) * 32 + ((r >> 3) & 1) * 16 + ((r >> 4) & 3) * 4 + (r >> 6))
-    wide = [jnp.broadcast_to(wo_ref[min(c, 2) : min(c, 2) + 1, :].astype(F32), (HALF, C)) for c in range(4)]
+    zero_row = jnp.zeros((width, C), BF)
+    for w in range(TW):
+        xt_ref[w, 0] = zero_row
+        xt_ref[w, TH + 1] = zero_row
+    wo_copy.wait()
+    wide = [jnp.broadcast_to(wo_buf[min(c, 2) : min(c, 2) + 1, :].astype(F32), (HALF, C)) for c in range(4)]
     proj_ref[...] = jnp.concatenate(wide, axis=0).T.astype(BF)
-    zero_row = jnp.zeros((width, C), BF)
-    for w in range(TW):
-        xt[w, 0] = zero_row
-        xt[w, TH + 1] = zero_row
     for b in range(blocks):
+        x_copies[b].wait()
         for part in range(TH // 4):
             rows = jnp.concatenate(
                 [
-                    x_ref[b * GB + g, f * HALF + part * 16 : f * HALF + part * 16 + 16, :]
+                    slab[b * GB + g, f * HALF + part * 16 : f * HALF + part * 16 + 16, :]
                     for g in range(GB)
                     for f in range(FC)
                 ],
@@ -103,7 +72,49 @@
             )
             moved = dot(perm, rows).astype(BF)
             for w in range(TW):
-                xt[w, 1 + part * 4 : 5 + part * 4, b * GF : (b + 1) * GF] = moved[w * 64 : w * 64 + 64].reshape(4, GF, C)
+                xt_ref[w, 1 + part * 4 : 5 + part * 4, b * GF : (b + 1) * GF] = moved[w * 64 : w * 64 + 64].reshape(
+                    4, GF, C
+                )
+    even = even_ref[0]
+    for out_ref, row in ((a_ref, 1 + even * (TH - 1)), (b_ref, TH - even * (TH - 1))):
+        for w in range(TW):
+            out_ref[w * width : (w + 1) * width, :] = xt_ref[w, row]
+    ws_copy.wait()
+
+
+def prep(even, latents, ws, wo):
+    groups = latents.shape[0]
+    width = groups * FC
+    vmem = pl.BlockSpec(memory_space=pltpu.VMEM)
+    hbm = pl.BlockSpec(memory_space=pltpu.HBM)
+    return pl.pallas_call(
+        prep_kernel,
+        out_shape=(
+            jax.ShapeDtypeStruct((TW * width, C), BF),
+            jax.ShapeDtypeStruct((TW * width, C), BF),
+            jax.ShapeDtypeStruct((TW, TH + 2, width, C), BF),
+            jax.ShapeDtypeStruct(ws.shape, BF),
+            jax.ShapeDtypeStruct((C, 4 * HALF), BF),
+        ),
+        in_specs=[pl.BlockSpec(memory_space=pltpu.SMEM)] + [hbm] * 3,
+        out_specs=(vmem,) * 5,
+        scratch_shapes=[
+            pltpu.VMEM(latents.shape, BF),
+            pltpu.VMEM(wo.shape, BF),
+            pltpu.SemaphoreType.DMA((groups // GB + 2,)),
+        ],
+        compiler_params=pltpu.CompilerParams(vmem_limit_bytes=32 * 1024 * 1024),
+        cost_estimate=pl.CostEstimate(flops=400_000_000, bytes_accessed=3_200_000, transcendentals=0),
+        name="prep",
+    )(even, *(pltpu.with_memory_space_constraint(a, pltpu.HBM) for a in (latents, ws, wo)))
+
+
+def main_kernel(xt, ws_ref, wt_hbm, proj_ref, rim_ref, field_ref, sums_ref, wt_ref, act, mix, sem):
+    wt_copy = pltpu.make_async_copy(wt_hbm, wt_ref, sem)
+    wt_copy.start()
+    width = xt.shape[2]
+    blocks = width // GF
+    half = blocks * GB
     inner = TH - 2
     for w in range(TW):
         taps = [(dy, dx) for dx in range(3) if 0 <= w + dx - 1 < TW for dy in range(3)]
@@ -117,6 +128,7 @@
         live = silu(total[1 : TH - 1].reshape(inner * width, C)).reshape(inner * blocks, FC, GB, C)
         for f in range(FC):
             act[w, :, f * C : (f + 1) * C] = live[:, f].reshape(inner * half, C).astype(BF)
+    wt_copy.wait()
     for w in range(TW):
         temporal = dot(act[w], temporal_matrix(wt_ref))
         field = xt[w, 2:TH].astype(F32).reshape(inner * blocks, FC, GB, C)
@@ -137,9 +149,9 @@
             sums_ref[b, f] = sums[b][f]
 
 
-def main(latents, ws, wt, wo):
-    groups = latents.shape[0]
-    width = groups * FC
+def main(xt, ws, wt, proj):
+    width = xt.shape[2]
+    groups = width // FC
     vmem = pl.BlockSpec(memory_space=pltpu.VMEM)
     return pl.pallas_call(
         main_kernel,
@@ -147,19 +159,19 @@
             jax.ShapeDtypeStruct((2, TW, width, C), F32),
             jax.ShapeDtypeStruct((2, TW, width, C), BF),
             jax.ShapeDtypeStruct((groups // GB, FC, GB, 4 * HALF), F32),
-            jax.ShapeDtypeStruct((C, 4 * HALF), BF),
+            jax.ShapeDtypeStruct(wt.shape, BF),
         ),
-        in_specs=[vmem] * 4,
+        in_specs=[vmem, vmem, pl.BlockSpec(memory_space=pltpu.HBM), vmem],
         out_specs=(vmem,) * 4,
         scratch_shapes=[
-            pltpu.VMEM((TW, TH + 2, width, C), BF),
             pltpu.VMEM((TW, (TH - 2) * groups, FC * C), BF),
             pltpu.VMEM((TW, FC, (TH - 2) * groups, C), BF),
+            pltpu.SemaphoreType.DMA,
         ],
         compiler_params=pltpu.CompilerParams(vmem_limit_bytes=32 * 1024 * 1024),
-        cost_estimate=pl.CostEstimate(flops=5_000_000_000, bytes_accessed=4_500_000, transcendentals=700_000),
+        cost_estimate=pl.CostEstimate(flops=4_500_000_000, bytes_accessed=4_500_000, transcendentals=700_000),
         name="main",
-    )(latents, ws, wt, wo)
+    )(xt, ws, pltpu.with_memory_space_constraint(wt, pltpu.HBM), proj)
 
 
 def finish_kernel(
@@ -211,7 +223,8 @@
     slots = out_ref.shape[0] // 8
     row = lax.broadcasted_iota(jnp.int32, (slots, count), 0) // 3
     group = lax.broadcasted_iota(jnp.int32, (slots, count), 1)
-    named = jnp.broadcast_to(owners_ref[...], (slots, count)) == row // 2
+    streams = slots // 6
+    named = jnp.broadcast_to(owners_ref[...], (slots, count)) == (row // 2 + streams // 2) % streams
     earlier = lax.broadcasted_iota(jnp.int32, (count, count), 0) < lax.broadcasted_iota(jnp.int32, (count, count), 1)
     rank = dot(named.astype(F32).astype(BF), earlier.astype(F32).astype(BF)).astype(jnp.int32)
     placed = named & (rank == row % 2) & (group < live_ref[0])
@@ -241,22 +254,27 @@
     latents = latents.reshape(groups, CELLS, C)
     streams, bands = lax.axis_size("stream"), lax.axis_size("band")
     even = (1 - (lax.axis_index("tile") & 1)).reshape(1)
-    send_a, send_b = edges(even, latents)
+    send_a, send_b, xt, ws, proj = prep(even, latents, spatial_weight, out_weight)
     side_b = lax.ppermute(send_b, "tile", [(1, 2), (2, 1)])
     side_a = lax.ppermute(send_a, "tile", [(0, 1), (1, 0), (2, 3), (3, 2)])
-    rim, field, sums, proj = main(latents, spatial_weight, temporal_weight, out_weight)
+    rim, field, sums, wt = main(xt, ws, temporal_weight, proj)
     rows = bands * streams * 2 * 3
-    outgoing = finish(
-        even, live_counts, side_a, side_b, rim, field, sums, proj, spatial_weight, temporal_weight,
-        owners.reshape(1, groups), rows,
+    outgoing = finish(even, live_counts, side_a, side_b, rim, field, sums, proj, ws, wt, owners.reshape(1, groups), rows)
+    band_list = list(range(bands))[::-1]
+    stream_list = list(range(streams // 2, streams)) + list(range(streams // 2))
+    parity = lax.axis_index("band")
+    signs = 1 - 2 * (lax.population_count(parity & (bands - 1 - jnp.arange(bands, dtype=jnp.int32))) & 1)
+    signs = signs.astype(F32) * F32(8.0**-0.5)
+    outgoing, signs = lax.optimization_barrier((outgoing.reshape(bands, streams * 6, CELLS), signs))
+    got = lax.all_to_all(
+        outgoing, "band", split_axis=0, concat_axis=0, tiled=True, axis_index_groups=[band_list]
     )
-    parity = lax.axis_index("band")
-    signs = 1 - 2 * (lax.population_count(parity & jnp.arange(bands, dtype=jnp.int32)) & 1)
-    signs = signs.astype(F32) * F32(8.0**-0.5)
-    outgoing, signs = lax.optimization_barrier((outgoing.reshape(rows // 2, 2, CELLS), signs))
-    got = lax.all_to_all(outgoing, ("band", "stream"), split_axis=0, concat_axis=0, tiled=True)
-    got = got.reshape(bands, streams * 2 * 3, CELLS).astype(F32)
-    frames = jnp.sum(got * signs[:, None, None], axis=0)
+    frames = jnp.sum(got.astype(F32) * signs[:, None, None], axis=0)
+    frames = lax.optimization_barrier(frames.reshape(streams * 3, 2, CELLS))
+    frames = lax.all_to_all(
+        frames, "stream", split_axis=0, concat_axis=0, tiled=True, axis_index_groups=[stream_list]
+    )
+    frames = jnp.roll(frames.reshape(streams, 6, CELLS), streams // 2, axis=0)
     return frames.reshape(streams * 2, 1, 3, CELLS)
 
 

time: 60 us -> 48.1 us (0.80)
  blocking collectives: 37.5 us -> 28.1 us
  local copies, waits for them, and re-layouts: 2.28 us -> 0.72 us
  other arithmetic: 0.74 us -> 0.13 us
    all_to_all x1 -> x2, blocking collectives: 37.5 us -> 28.1 us  [the longest x1 18 us: local(): lax.all_to_all(frames, 'stream', split_axis=0, concat_axis=0, tiled=True,...]
    unnamed x12 -> x2, local copies, waits for them, and re-layouts: 2.28 us -> 0.01 us
    reshape x0 -> x1, local copies, waits for them, and re-layouts: none -> 0.67 us  [local(): return frames.reshape(streams * 2, 1, 3, CELLS)]
    reduce_sum x1, other arithmetic: 0.72 us -> 0.1 us  [local(): frames = jnp.sum(got.astype(F32) * signs[:, None, None], axis=0)]
  transfers between devices with their start and end apart: 2 -> 2, of which waited for: 0 -> 0; matrix products, arithmetic and copies ran while one was open for 0% -> 0% of each run, Pallas kernels for 8% -> 9%
where the time goes in v3:
time: 48.1 us; the launch traced here: 47.9 us
  blocking collectives  28.1 us (58%)
  starting transfers between devices  10.7 us (22%)
  Pallas kernels  7.45 us (15%)
  between operations  0.74 us (2%)
  local copies, waits for them, and re-layouts  0.72 us (1%)
    all_to_all x1, blocking collectives, local(): lax.all_to_all(frames, 'stream', split_axis=0, concat_axis=0, tiled=True,...  18 us
    all_to_all x1, blocking collectives, local(): lax.all_to_all(outgoing, 'band', split_axis=0, concat_axis=0, tiled=True,...  10.1 us
    ppermute x1, starting transfers between devices, local(): side_a = lax.ppermute(send_a, 'tile', [(0, 1), (1, 0), (2, 3), (3, 2)])  8.79 us
    pallas_call x1, Pallas kernels, main(): pl.pallas_call(main_kernel, out_shape=(jax.ShapeDtypeStruct((2, TW, width...  4.52 us
    pallas_call x1, Pallas kernels, prep(): pl.pallas_call(prep_kernel, out_shape=(jax.ShapeDtypeStruct((TW * width,...  2.02 us
    ppermute x1, starting transfers between devices, local(): side_b = lax.ppermute(send_b, 'tile', [(1, 2), (2, 1)])  1.92 us
  transfers between devices with their start and end apart: 2, of which 0 were waited for; matrix products, arithmetic and copies ran while one was open for 0% of the time, Pallas kernels for 9%

profile of v3, /device:TPU:1, one launch (start us, length us, event | category | flops | bytes accessed | tf_op | source)
XLA Modules:
  0.0 47.9 jit_solution(17404375537530820591)
XLA Ops:
  0.0 2.0 %prep.1 = (bf16[192,256]{1,0:T(8,128)(2,1)S(1)}, bf16[192,256]{1,0:T(8,128)(2,1)S(1)}, bf16[4,18,48,256]{3,2,1,0:T(8,128)(2,1)S(1)}, bf16[3,3,256,256]{3,2,1,0:T(8,128)(2,1)S(1)}, bf16[256,256]{1,0:T(8,128)(2,1)S(1)}) custom-call(s32[1]{0:T(128)} %bitcast.even_ref, bf16[24,128,256]{2,1,0:T(8,128)(2,1)} %bitcast.7, bf16[3,3,256,256]{3,2,1,0:T(8,128)(2,1)} %ws_ref.1, ...), custom_call_target="tpu_custom_call" | custom-call | flops 400000000 | bytes 3200000 | tf_op jit(solution)/shard_map/prep/pallas_call | solution.py:90
  2.0 8.8 %collective-permute-start = (bf16[192,256]{1,0:T(8,128)(2,1)S(1)}, bf16[192,256]{1,0:T(8,128)(2,1)S(1)}, u32[]{:S(2)}, u32[]{:S(2)}) collective-permute-start(bf16[192,256]{1,0:T(8,128)(2,1)S(1)} %get-tuple-element.16), channel_id=1, source_target_pairs={{0,8},{8,0},{16,24},{24,16},{1,9},{9,1},{17,25},{25,17},{2,10},{10... | collective-permute-start | bytes 294920 | tf_op jit(solution)/shard_map/ppermute | solution.py:259
  10.8 1.9 %collective-permute-start.1 = (bf16[192,256]{1,0:T(8,128)(2,1)S(1)}, bf16[192,256]{1,0:T(8,128)(2,1)S(1)}, u32[]{:S(2)}, u32[]{:S(2)}) collective-permute-start(bf16[192,256]{1,0:T(8,128)(2,1)S(1)} %get-tuple-element.17), channel_id=1, source_target_pairs={{8,16},{16,8},{9,17},{17,9},{10,18},{18,10},{11,19},{19,11},{12,20... | collective-permute-start | bytes 294920 | tf_op jit(solution)/shard_map/ppermute | solution.py:258
  13.4 0.0 copy-start
  13.4 4.5 %main.1 = (f32[2,4,48,256]{3,2,1,0:T(8,128)S(1)}, bf16[2,4,48,256]{3,2,1,0:T(8,128)(2,1)S(1)}, f32[3,2,8,256]{3,2,1,0:T(8,128)S(1)}, bf16[3,256,256]{2,1,0:T(8,128)(2,1)S(1)}) custom-call(bf16[4,18,48,256]{3,2,1,0:T(8,128)(2,1)S(1)} %get-tuple-element.18.xt, bf16[3,3,256,256]{3,2,1,0:T(8,128)(2,1)S(1)} %get-tuple-element.19.ws_ref, ...), custom_call_target="tpu_custom_call" | custom-call | flops 4499999744 | bytes 4500000 | tf_op jit(solution)/shard_map/main/pallas_call | solution.py:156
  18.0 0.0 collective-permute-done.a_ref
  18.0 0.0 collective-permute-done.1.b_ref
  18.0 0.0 copy-done
  18.0 0.9 %finish.1 = bf16[768,128]{1,0:T(8,128)(2,1)S(1)} custom-call(s32[1]{0:T(128)} %bitcast.even_ref, s32[1]{0:T(128)S(6)} %copy.8.live_ref, bf16[192,256]{1,0:T(8,128)(2,1)S(1)} %collective-permute-done.a_ref, bf16[192,256]{1,0:T(8,128)(2,1)S(1)} %collective-permute-done.1.b_ref, f32[2,4,48,256]{3,2,1,0:T(8,128)S(1)} %get-tuple-element.21.rim_ref, ...), custom_call_target="tpu_custom_call" | custom-call | flops 500000000 | bytes 3000000 | tf_op jit(solution)/shard_map/finish/pallas_call | solution.py:241
  18.9 10.1 %all_to_all.10 = bf16[8,96,128]{2,1,0:T(8,128)(2,1)S(1)} all-to-all(bf16[8,96,128]{2,1,0:T(8,128)(2,1)S(1)} %bitcast.5), channel_id=1, replica_groups={{7,6,5,4,3,2,1,0},{15,14,13,12,11,10,9,8},{23,22,21,20,19,18,17,16},{31..., dimensions={0} | all-to-all | bytes 393216 | tf_op jit(solution)/shard_map/all_to_all | solution.py:269
  29.0 0.1 multiply_reduce_fusion
  29.1 18.0 %all_to_all.11 = f32[48,2,128]{2,1,0:T(2,128)S(1)} all-to-all(f32[48,2,128]{2,1,0:T(2,128)S(1)} %bitcast.8), channel_id=1, replica_groups={{256,288,320,352,384,416,448,480,0,32,64,96,128,160,192,224},{257,289,3..., dimensions={0} | all-to-all | bytes 98304 | tf_op jit(solution)/shard_map/all_to_all | solution.py:274
  47.2 0.7 %reshape.28 = f32[32,1,3,128]{3,1,2,0:T(1,128)} reshape(f32[16,6,128]{2,1,0:T(8,128)S(1)} %pad_maximum_fusion) | data formatting | bytes 98304 | tf_op jit(solution)/shard_map/reshape | solution.py:278
  (5 shorter events, 0.1 us)
Async XLA Ops:
  2.0 15.9 %collective-permute-start = (bf16[192,256]{1,0:T(8,128)(2,1)S(1)}, bf16[192,256]{1,0:T(8,128)(2,1)S(1)}, u32[]{:S(2)}, u32[]{:S(2)}) collective-permute-start(bf16[192,256]{1,0:T(8,128)(2,1)S(1)} %get-tuple-element.16), channel_id=1, source_target_pairs={{0,8},{8,0},{16,24},{24,16},{1,9},{9,1},{17,25},{25,17},{2,10},{10... | collective-permute-start | bytes 294920 | tf_op jit(solution)/shard_map/ppermute | solution.py:259
  10.8 7.1 %collective-permute-start.1 = (bf16[192,256]{1,0:T(8,128)(2,1)S(1)}, bf16[192,256]{1,0:T(8,128)(2,1)S(1)}, u32[]{:S(2)}, u32[]{:S(2)}) collective-permute-start(bf16[192,256]{1,0:T(8,128)(2,1)S(1)} %get-tuple-element.17), channel_id=1, source_target_pairs={{8,16},{16,8},{9,17},{17,9},{10,18},{18,10},{11,19},{19,11},{12,20... | collective-permute-start | bytes 294920 | tf_op jit(solution)/shard_map/ppermute | solution.py:258
  13.4 4.6 %copy-start = (s32[24,1]{0,1:T(1,128)S(1)}, s32[24,1]{0,1:T(1,128)}, u32[]{:S(2)}) copy-start(s32[24,1]{0,1:T(1,128)} %param.7) | copy-start | bytes 292

commit v4 on v3

--- a/solution.py
+++ b/solution.py
@@ -26,9 +26,8 @@
 
 
 def one_hot(rows, cols, place):
-    row = lax.broadcasted_iota(jnp.int32, (rows, cols), 0)
-    col = lax.broadcasted_iota(jnp.int32, (rows, cols), 1)
-    return (place(row) == col).astype(F32).astype(BF)
+    wanted = jnp.broadcast_to(place(lax.broadcasted_iota(jnp.int32, (rows, 1), 0)), (rows, cols))
+    return jnp.where(wanted == lax.broadcasted_iota(jnp.int32, (rows, cols), 1), 1.0, 0.0).astype(BF)
 
 
 def temporal_matrix(wt_ref):
@@ -38,7 +37,7 @@
 
 
 def prep_kernel(
-    even_ref, x_ref, ws_ref, wo_ref, a_ref, b_ref, xt_ref, ws_out, proj_ref, slab, wo_buf, sems
+    even_ref, x_ref, ws_ref, a_ref, b_ref, xt_ref, ws_out, slab, sems
 ):
     groups = x_ref.shape[0]
     blocks = groups // GB
@@ -47,18 +46,14 @@
         pltpu.make_async_copy(x_ref.at[b * GB : (b + 1) * GB], slab.at[b * GB : (b + 1) * GB], sems.at[b])
         for b in range(blocks)
     ]
-    wo_copy = pltpu.make_async_copy(wo_ref, wo_buf, sems.at[blocks])
-    ws_copy = pltpu.make_async_copy(ws_ref, ws_out, sems.at[blocks + 1])
-    for copy in [wo_copy] + x_copies + [ws_copy]:
+    ws_copy = pltpu.make_async_copy(ws_ref, ws_out, sems.at[blocks])
+    for copy in x_copies + [ws_copy]:
         copy.start()
     perm = one_hot(256, 256, lambda r: (r & 7) * 32 + ((r >> 3) & 1) * 16 + ((r >> 4) & 3) * 4 + (r >> 6))
     zero_row = jnp.zeros((width, C), BF)
     for w in range(TW):
         xt_ref[w, 0] = zero_row
         xt_ref[w, TH + 1] = zero_row
-    wo_copy.wait()
-    wide = [jnp.broadcast_to(wo_buf[min(c, 2) : min(c, 2) + 1, :].astype(F32), (HALF, C)) for c in range(4)]
-    proj_ref[...] = jnp.concatenate(wide, axis=0).T.astype(BF)
     for b in range(blocks):
         x_copies[b].wait()
         for part in range(TH // 4):
@@ -82,7 +77,7 @@
     ws_copy.wait()
 
 
-def prep(even, latents, ws, wo):
+def prep(even, latents, ws):
     groups = latents.shape[0]
     width = groups * FC
     vmem = pl.BlockSpec(memory_space=pltpu.VMEM)
@@ -94,24 +89,27 @@
             jax.ShapeDtypeStruct((TW * width, C), BF),
             jax.ShapeDtypeStruct((TW, TH + 2, width, C), BF),
             jax.ShapeDtypeStruct(ws.shape, BF),
-            jax.ShapeDtypeStruct((C, 4 * HALF), BF),
         ),
-        in_specs=[pl.BlockSpec(memory_space=pltpu.SMEM)] + [hbm] * 3,
-        out_specs=(vmem,) * 5,
+        in_specs=[pl.BlockSpec(memory_space=pltpu.SMEM)] + [hbm] * 2,
+        out_specs=(vmem,) * 4,
         scratch_shapes=[
             pltpu.VMEM(latents.shape, BF),
-            pltpu.VMEM(wo.shape, BF),
-            pltpu.SemaphoreType.DMA((groups // GB + 2,)),
+            pltpu.SemaphoreType.DMA((groups // GB + 1,)),
         ],
         compiler_params=pltpu.CompilerParams(vmem_limit_bytes=32 * 1024 * 1024),
         cost_estimate=pl.CostEstimate(flops=400_000_000, bytes_accessed=3_200_000, transcendentals=0),
         name="prep",
-    )(even, *(pltpu.with_memory_space_constraint(a, pltpu.HBM) for a in (latents, ws, wo)))
-
-
-def main_kernel(xt, ws_ref, wt_hbm, proj_ref, rim_ref, field_ref, sums_ref, wt_ref, act, mix, sem):
+    )(even, *(pltpu.with_memory_space_constraint(a, pltpu.HBM) for a in (latents, ws)))
+
+
+def main_kernel(xt, ws_ref, wt_hbm, wo_ref, rim_ref, field_ref, sums_ref, wt_ref, proj_ref, act, mix, sem):
     wt_copy = pltpu.make_async_copy(wt_hbm, wt_ref, sem)
     wt_copy.start()
+    channel = lax.broadcasted_iota(jnp.int32, (wo_ref.shape[0], 4 * HALF), 1) // HALF
+    spread = (channel == lax.broadcasted_iota(jnp.int32, channel.shape, 0)).astype(F32)
+    proj_ref[...] = lax.dot_general(
+        wo_ref[...].astype(F32), spread, (((0,), (0,)), ((), ())), preferred_element_type=F32
+    ).astype(BF)
     width = xt.shape[2]
     blocks = width // GF
     half = blocks * GB
@@ -149,7 +147,7 @@
             sums_ref[b, f] = sums[b][f]
 
 
-def main(xt, ws, wt, proj):
+def main(xt, ws, wt, wo):
     width = xt.shape[2]
     groups = width // FC
     vmem = pl.BlockSpec(memory_space=pltpu.VMEM)
@@ -160,9 +158,10 @@
             jax.ShapeDtypeStruct((2, TW, width, C), BF),
             jax.ShapeDtypeStruct((groups // GB, FC, GB, 4 * HALF), F32),
             jax.ShapeDtypeStruct(wt.shape, BF),
+            jax.ShapeDtypeStruct((C, 4 * HALF), BF),
         ),
         in_specs=[vmem, vmem, pl.BlockSpec(memory_space=pltpu.HBM), vmem],
-        out_specs=(vmem,) * 4,
+        out_specs=(vmem,) * 5,
         scratch_shapes=[
             pltpu.VMEM((TW, (TH - 2) * groups, FC * C), BF),
             pltpu.VMEM((TW, FC, (TH - 2) * groups, C), BF),
@@ -171,7 +170,7 @@
         compiler_params=pltpu.CompilerParams(vmem_limit_bytes=32 * 1024 * 1024),
         cost_estimate=pl.CostEstimate(flops=4_500_000_000, bytes_accessed=4_500_000, transcendentals=700_000),
         name="main",
-    )(xt, ws, pltpu.with_memory_space_constraint(wt, pltpu.HBM), proj)
+    )(xt, ws, pltpu.with_memory_space_constraint(wt, pltpu.HBM), wo)
 
 
 def finish_kernel(
@@ -220,7 +219,7 @@
                 first = pltpu.roll(first, HALF, 1)
             channels.append(jnp.where(narrow, first, second))
     stacked = jnp.concatenate(channels, axis=0).astype(BF)
-    slots = out_ref.shape[0] // 8
+    slots = out_ref.shape[0]
     row = lax.broadcasted_iota(jnp.int32, (slots, count), 0) // 3
     group = lax.broadcasted_iota(jnp.int32, (slots, count), 1)
     streams = slots // 6
@@ -231,8 +230,7 @@
     channel = lax.broadcasted_iota(jnp.int32, (slots, count), 0) % 3
     placing = jnp.concatenate([(placed & (channel == c)).astype(F32) for c in range(3)], axis=1).astype(BF)
     message = dot(placing, stacked).astype(BF)
-    for p in range(8):
-        out_ref[p * slots : (p + 1) * slots, :] = message
+    out_ref[...] = message
 
 
 def finish(even, live, side_a, side_b, rim, field, sums, proj, ws, wt, owners, rows):
@@ -254,27 +252,26 @@
     latents = latents.reshape(groups, CELLS, C)
     streams, bands = lax.axis_size("stream"), lax.axis_size("band")
     even = (1 - (lax.axis_index("tile") & 1)).reshape(1)
-    send_a, send_b, xt, ws, proj = prep(even, latents, spatial_weight, out_weight)
+    send_a, send_b, xt, ws = prep(even, latents, spatial_weight)
     side_b = lax.ppermute(send_b, "tile", [(1, 2), (2, 1)])
     side_a = lax.ppermute(send_a, "tile", [(0, 1), (1, 0), (2, 3), (3, 2)])
-    rim, field, sums, wt = main(xt, ws, temporal_weight, proj)
-    rows = bands * streams * 2 * 3
+    rim, field, sums, wt, proj = main(xt, ws, temporal_weight, out_weight)
+    rows = streams * 2 * 3
     outgoing = finish(even, live_counts, side_a, side_b, rim, field, sums, proj, ws, wt, owners.reshape(1, groups), rows)
-    band_list = list(range(bands))[::-1]
+    band_list = [6, 7, 5, 4, 3, 2, 1, 0]
     stream_list = list(range(streams // 2, streams)) + list(range(streams // 2))
     parity = lax.axis_index("band")
-    signs = 1 - 2 * (lax.population_count(parity & (bands - 1 - jnp.arange(bands, dtype=jnp.int32))) & 1)
+    signs = 1 - 2 * (lax.population_count(parity & jnp.array(band_list, dtype=jnp.int32)) & 1)
     signs = signs.astype(F32) * F32(8.0**-0.5)
-    outgoing, signs = lax.optimization_barrier((outgoing.reshape(bands, streams * 6, CELLS), signs))
+    outgoing, signs = lax.optimization_barrier((outgoing.reshape(streams * 3, 2, CELLS), signs))
     got = lax.all_to_all(
-        outgoing, "band", split_axis=0, concat_axis=0, tiled=True, axis_index_groups=[band_list]
+        outgoing, "stream", split_axis=0, concat_axis=0, tiled=True, axis_index_groups=[stream_list]
     )
+    half = streams * 3 // 2
+    got = jnp.concatenate([got[half:], got[:half]], axis=0).reshape(1, rows, CELLS)
+    got = lax.optimization_barrier(jnp.broadcast_to(got, (bands, rows, CELLS)))
+    got = lax.all_to_all(got, "band", split_axis=0, concat_axis=0, tiled=True, axis_index_groups=[band_list])
     frames = jnp.sum(got.astype(F32) * signs[:, None, None], axis=0)
-    frames = lax.optimization_barrier(frames.reshape(streams * 3, 2, CELLS))
-    frames = lax.all_to_all(
-        frames, "stream", split_axis=0, concat_axis=0, tiled=True, axis_index_groups=[stream_list]
-    )
-    frames = jnp.roll(frames.reshape(streams, 6, CELLS), streams // 2, axis=0)
     return frames.reshape(streams * 2, 1, 3, CELLS)
 
 

time: 48.1 us -> 46.9 us (0.975)
  blocking collectives: 28.1 us -> 26.7 us
  local copies, waits for them, and re-layouts: 0.72 us -> 0.06 us
  other arithmetic: 0.13 us -> 0.78 us
    all_to_all x2, blocking collectives: 28.1 us -> 26.7 us  [the longest x1 15.9 us: local(): lax.all_to_all(outgoing, 'stream', split_axis=0, concat_axis=0, tiled=Tru...]
    reshape x1 -> x0, local copies, waits for them, and re-layouts: 0.67 us -> none  [local(): return frames.reshape(streams * 2, 1, 3, CELLS)]
    reduce_sum x1, other arithmetic: 0.1 us -> 0.72 us  [local(): frames = jnp.sum(got.astype(F32) * signs[:, None, None], axis=0)]
  transfers between devices with their start and end apart: 2 -> 2, of which waited for: 0 -> 0; matrix products, arithmetic and copies ran while one was open for 0% -> 0% of each run, Pallas kernels for 9% -> 10%
where the time goes in v4:
time: 46.9 us; the launch traced here: 46.5 us
  blocking collectives  26.7 us (57%)
  starting transfers between devices  10.7 us (23%)
  Pallas kernels  7.51 us (16%)
  other arithmetic  0.78 us (2%)
  between operations  0.76 us (2%)
    all_to_all x1, blocking collectives, local(): lax.all_to_all(outgoing, 'stream', split_axis=0, concat_axis=0, tiled=Tru...  15.9 us
    all_to_all x1, blocking collectives, local(): lax.all_to_all(got, 'band', split_axis=0, concat_axis=0, tiled=True, axis...  10.8 us
    ppermute x1, starting transfers between devices, local(): side_a = lax.ppermute(send_a, 'tile', [(0, 1), (1, 0), (2, 3), (3, 2)])  8.79 us
    pallas_call x1, Pallas kernels, main(): pl.pallas_call(main_kernel, out_shape=(jax.ShapeDtypeStruct((2, TW, width...  4.6 us
    pallas_call x1, Pallas kernels, prep(): pl.pallas_call(prep_kernel, out_shape=(jax.ShapeDtypeStruct((TW * width,...  2.01 us
    ppermute x1, starting transfers between devices, local(): side_b = lax.ppermute(send_b, 'tile', [(1, 2), (2, 1)])  1.92 us
  transfers between devices with their start and end apart: 2, of which 0 were waited for; matrix products, arithmetic and copies ran while one was open for 0% of the time, Pallas kernels for 10%

profile of v4, /device:TPU:1, one launch (start us, length us, event | category | flops | bytes accessed | tf_op | source)
XLA Modules:
  0.0 46.5 jit_solution(5748174177675170996)
XLA Ops:
  0.0 0.0 copy-start.1
  0.0 2.0 %prep.1 = (bf16[192,256]{1,0:T(8,128)(2,1)S(1)}, bf16[192,256]{1,0:T(8,128)(2,1)S(1)}, bf16[4,18,48,256]{3,2,1,0:T(8,128)(2,1)S(1)}, bf16[3,3,256,256]{3,2,1,0:T(8,128)(2,1)S(1)}) custom-call(s32[1]{0:T(128)} %bitcast.even_ref, bf16[24,128,256]{2,1,0:T(8,128)(2,1)} %bitcast.8, bf16[3,3,256,256]{3,2,1,0:T(8,128)(2,1)} %ws_ref.1), custom_call_target="tpu_custom_call" | custom-call | flops 400000000 | bytes 3200000 | tf_op jit(solution)/shard_map/prep/pallas_call | solution.py:85
  2.0 8.8 %collective-permute-start = (bf16[192,256]{1,0:T(8,128)(2,1)S(1)}, bf16[192,256]{1,0:T(8,128)(2,1)S(1)}, u32[]{:S(2)}, u32[]{:S(2)}) collective-permute-start(bf16[192,256]{1,0:T(8,128)(2,1)S(1)} %get-tuple-element.16), channel_id=1, source_target_pairs={{0,8},{8,0},{16,24},{24,16},{1,9},{9,1},{17,25},{25,17},{2,10},{10... | collective-permute-start | bytes 294920 | tf_op jit(solution)/shard_map/ppermute | solution.py:257
  10.8 1.9 %collective-permute-start.1 = (bf16[192,256]{1,0:T(8,128)(2,1)S(1)}, bf16[192,256]{1,0:T(8,128)(2,1)S(1)}, u32[]{:S(2)}, u32[]{:S(2)}) collective-permute-start(bf16[192,256]{1,0:T(8,128)(2,1)S(1)} %get-tuple-element.17), channel_id=1, source_target_pairs={{8,16},{16,8},{9,17},{17,9},{10,18},{18,10},{11,19},{19,11},{12,20... | collective-permute-start | bytes 294920 | tf_op jit(solution)/shard_map/ppermute | solution.py:256
  12.7 0.0 copy-done.1
  12.8 0.0 copy-start.2
  12.8 0.0 copy-start
  12.8 4.6 %main.1 = (f32[2,4,48,256]{3,2,1,0:T(8,128)S(1)}, bf16[2,4,48,256]{3,2,1,0:T(8,128)(2,1)S(1)}, f32[3,2,8,256]{3,2,1,0:T(8,128)S(1)}, bf16[3,256,256]{2,1,0:T(8,128)(2,1)S(1)}, bf16[256,256]{1,0:T(8,128)(2,1)S(1)}) custom-call(bf16[4,18,48,256]{3,2,1,0:T(8,128)(2,1)S(1)} %get-tuple-element.18.xt, bf16[3,3,256,256]{3,2,1,0:T(8,128)(2,1)S(1)} %get-tuple-element.19.ws_ref, ...), custom_call_target="tpu_custom_call" | custom-call | flops 4499999744 | bytes 4500000 | tf_op jit(solution)/shard_map/main/pallas_call | solution.py:154
  17.4 0.0 copy-done.2
  18.1 0.0 collective-permute-done.a_ref
  18.1 0.0 collective-permute-done.1.b_ref
  18.1 0.0 copy-done
  18.1 0.9 %finish.1 = bf16[96,128]{1,0:T(8,128)(2,1)S(1)} custom-call(s32[1]{0:T(128)} %bitcast.even_ref, s32[1]{0:T(128)S(6)} %copy.10.live_ref, bf16[192,256]{1,0:T(8,128)(2,1)S(1)} %collective-permute-done.a_ref, bf16[192,256]{1,0:T(8,128)(2,1)S(1)} %collective-permute-done.1.b_ref, f32[2,4,48,256]{3,2,1,0:T(8,128)S(1)} %get-tuple-element.20.rim_ref, ...), custom_call_target="tpu_custom_call" | custom-call | flops 500000000 | bytes 3000000 | tf_op jit(solution)/shard_map/finish/pallas_call | solution.py:239
  19.0 15.9 %all_to_all.10 = bf16[48,2,128]{2,1,0:T(2,128)(2,1)S(1)} all-to-all(bf16[48,2,128]{2,1,0:T(2,128)(2,1)S(1)} %bitcast.6), channel_id=1, replica_groups={{256,288,320,352,384,416,448,480,0,32,64,96,128,160,192,224},{257,289,3..., dimensions={0} | all-to-all | bytes 49152 | tf_op jit(solution)/shard_map/all_to_all | solution.py:267
  35.0 10.8 %all_to_all.11 = bf16[8,96,128]{2,1,0:T(8,128)(2,1)S(1)} all-to-all(bf16[8,96,128]{2,1,0:T(8,128)(2,1)S(1)} %broadcast_in_dim.9), channel_id=1, replica_groups={{6,7,5,4,3,2,1,0},{14,15,13,12,11,10,9,8},{22,23,21,20,19,18,17,16},{30..., dimensions={0} | all-to-all | bytes 393216 | tf_op jit(solution)/shard_map/all_to_all | solution.py:273
  45.8 0.7 %multiply_reduce_fusion = f32[96,128]{1,0:T(8,128)} fusion(bf16[8,96,128]{2,1,0:T(8,128)(2,1)S(1)} %all_to_all.11, f32[8]{0:T(128)S(1)} %convert_multiply_fusion), kind=kLoop, calls=%fused_computation | loop fusion | flops 282624 | bytes 245792 | tf_op jit(solution)/shard_map/reduce_sum | solution.py:274
  (4 shorter events, 0.1 us)
Async XLA Ops:
  0.0 12.7 %copy-start.1 = (bf16[3,256]{1,0:T(4,128)(2,1)S(1)}, bf16[3,256]{1,0:T(4,128)(2,1)}, u32[]{:S(2)}) copy-start(bf16[3,256]{1,0:T(4,128)(2,1)} %wo_ref.1) | copy-start | bytes 4612
  2.0 16.0 %collective-permute-start = (bf16[192,256]{1,0:T(8,128)(2,1)S(1)}, bf16[192,256]{1,0:T(8,128)(2,1)S(1)}, u32[]{:S(2)}, u32[]{:S(2)}) collective-permute-start(bf16[192,256]{1,0:T(8,128)(2,1)S(1)} %get-tuple-element.16), channel_id=1, source_target_pairs={{0,8},{8,0},{16,24},{24,16},{1,9},{9,1},{17,25},{25,17},{2,10},{10... | collective-permute-start | bytes 294920 | tf_op jit(solution)/shard_map/ppermute | solution.py:257
  10.8 7.3 %collective-permute-start.1 = (bf16[192,256]{1,0:T(8,128)(2,1)S(1)}, bf16[192,256]{1,0:T(8,128)(2,1)S(1)}, u32[]{:S(2)}, u32[]{:S(2)}) collective-permute-start(bf16[192,256]{1,0:T(8,128)(2,1)S(1)} %get-tuple-element.17), channel_id=1, source_target_pairs={{8,16},{16,8},{9,17},{17,9},{10,18},{18,10},{11,19},{19,11},{12,20... | collective-permute-start | bytes 294920 | tf_op jit(solution)/shard_map/ppermute | solution.py:256
  12.8 4.6 %copy-start.2 = (s32[8]{0:T(128)S(1)}, s32[8]{0:T(128)}, u32[]{:S(2)}) copy-start(s32[8]{0:T(128)} %constant.19.clone) | copy-start | bytes 100
  12.8 5.3 %copy-start = (s32[24,1]{0,1:T(1,128)S(1)}, s32[24,1]{0,1:T(1,128)}, u32[]{:S(2)}) copy-start(s32[24,1]{0,1:T(1,128)} %param.8) | copy-start | bytes 292

commit v5 on v4

--- a/solution.py
+++ b/solution.py
@@ -102,7 +102,10 @@
     )(even, *(pltpu.with_memory_space_constraint(a, pltpu.HBM) for a in (latents, ws)))
 
 
-def main_kernel(xt, ws_ref, wt_hbm, wo_ref, rim_ref, field_ref, sums_ref, wt_ref, proj_ref, act, mix, sem):
+def main_kernel(
+    live_ref, xt, ws_ref, wt_hbm, wo_ref, owners_ref, rim_ref, field_ref, sums_ref, wt_ref, proj_ref, placing_ref,
+    act, mix, sem,
+):
     wt_copy = pltpu.make_async_copy(wt_hbm, wt_ref, sem)
     wt_copy.start()
     channel = lax.broadcasted_iota(jnp.int32, (wo_ref.shape[0], 4 * HALF), 1) // HALF
@@ -113,9 +116,19 @@
     width = xt.shape[2]
     blocks = width // GF
     half = blocks * GB
+    slots, count = placing_ref.shape[0], half
+    row = lax.broadcasted_iota(jnp.int32, (slots, count), 0) // 3
+    group = lax.broadcasted_iota(jnp.int32, (slots, count), 1)
+    streams = slots // 6
+    named = jnp.broadcast_to(owners_ref[...], (slots, count)) == (row // 2 + streams // 2) % streams
+    earlier = lax.broadcasted_iota(jnp.int32, (count, count), 0) < lax.broadcasted_iota(jnp.int32, (count, count), 1)
+    rank = dot(named.astype(F32).astype(BF), earlier.astype(F32).astype(BF)).astype(jnp.int32)
+    placed = named & (rank == row % 2) & (group < live_ref[0])
+    channel = lax.broadcasted_iota(jnp.int32, (slots, count), 0) % 3
+    placing_ref[...] = jnp.concatenate([(placed & (channel == c)).astype(F32) for c in range(3)], axis=1).astype(BF)
     inner = TH - 2
     for w in range(TW):
-        taps = [(dy, dx) for dx in range(3) if 0 <= w + dx - 1 < TW for dy in range(3)]
+        taps = [(dy, dx) for dy in range(3) for dx in range(3) if 0 <= w + dx - 1 < TW]
         lhs = jnp.concatenate([xt[w + dx - 1, dy : dy + TH].reshape(TH * width, C) for dy, dx in taps], axis=1)
         rhs = jnp.concatenate([ws_ref[dy, dx] for dy, dx in taps], axis=0)
         total = dot(lhs, rhs).reshape(TH, width, C)
@@ -147,7 +160,7 @@
             sums_ref[b, f] = sums[b][f]
 
 
-def main(xt, ws, wt, wo):
+def main(live, xt, ws, wt, wo, owners, rows):
     width = xt.shape[2]
     groups = width // FC
     vmem = pl.BlockSpec(memory_space=pltpu.VMEM)
@@ -159,9 +172,12 @@
             jax.ShapeDtypeStruct((groups // GB, FC, GB, 4 * HALF), F32),
             jax.ShapeDtypeStruct(wt.shape, BF),
             jax.ShapeDtypeStruct((C, 4 * HALF), BF),
+            jax.ShapeDtypeStruct((rows, 3 * groups), BF),
         ),
-        in_specs=[vmem, vmem, pl.BlockSpec(memory_space=pltpu.HBM), vmem],
-        out_specs=(vmem,) * 5,
+        in_specs=[
+            pl.BlockSpec(memory_space=pltpu.SMEM), vmem, vmem, pl.BlockSpec(memory_space=pltpu.HBM), vmem, vmem
+        ],
+        out_specs=(vmem,) * 6,
         scratch_shapes=[
             pltpu.VMEM((TW, (TH - 2) * groups, FC * C), BF),
             pltpu.VMEM((TW, FC, (TH - 2) * groups, C), BF),
@@ -170,11 +186,11 @@
         compiler_params=pltpu.CompilerParams(vmem_limit_bytes=32 * 1024 * 1024),
         cost_estimate=pl.CostEstimate(flops=4_500_000_000, bytes_accessed=4_500_000, transcendentals=700_000),
         name="main",
-    )(xt, ws, pltpu.with_memory_space_constraint(wt, pltpu.HBM), wo)
+    )(live, xt, ws, pltpu.with_memory_space_constraint(wt, pltpu.HBM), wo, owners)
 
 
 def finish_kernel(
-    even_ref, live_ref, a_ref, b_ref, rim_ref, field_ref, sums_ref, proj_ref, ws_ref, wt_ref, owners_ref, out_ref
+    even_ref, a_ref, b_ref, rim_ref, field_ref, sums_ref, proj_ref, ws_ref, wt_ref, placing_ref, out_ref
 ):
     blocks = sums_ref.shape[0]
     count = blocks * GB
@@ -219,32 +235,21 @@
                 first = pltpu.roll(first, HALF, 1)
             channels.append(jnp.where(narrow, first, second))
     stacked = jnp.concatenate(channels, axis=0).astype(BF)
-    slots = out_ref.shape[0]
-    row = lax.broadcasted_iota(jnp.int32, (slots, count), 0) // 3
-    group = lax.broadcasted_iota(jnp.int32, (slots, count), 1)
-    streams = slots // 6
-    named = jnp.broadcast_to(owners_ref[...], (slots, count)) == (row // 2 + streams // 2) % streams
-    earlier = lax.broadcasted_iota(jnp.int32, (count, count), 0) < lax.broadcasted_iota(jnp.int32, (count, count), 1)
-    rank = dot(named.astype(F32).astype(BF), earlier.astype(F32).astype(BF)).astype(jnp.int32)
-    placed = named & (rank == row % 2) & (group < live_ref[0])
-    channel = lax.broadcasted_iota(jnp.int32, (slots, count), 0) % 3
-    placing = jnp.concatenate([(placed & (channel == c)).astype(F32) for c in range(3)], axis=1).astype(BF)
-    message = dot(placing, stacked).astype(BF)
-    out_ref[...] = message
-
-
-def finish(even, live, side_a, side_b, rim, field, sums, proj, ws, wt, owners, rows):
+    out_ref[...] = dot(placing_ref[...], stacked).astype(BF)
+
+
+def finish(even, side_a, side_b, rim, field, sums, proj, ws, wt, placing):
     vmem = pl.BlockSpec(memory_space=pltpu.VMEM)
     smem = pl.BlockSpec(memory_space=pltpu.SMEM)
     return pl.pallas_call(
         finish_kernel,
-        out_shape=jax.ShapeDtypeStruct((rows, CELLS), BF),
-        in_specs=[smem, smem] + [vmem] * 9,
+        out_shape=jax.ShapeDtypeStruct((placing.shape[0], CELLS), BF),
+        in_specs=[smem] + [vmem] * 9,
         out_specs=vmem,
         compiler_params=pltpu.CompilerParams(vmem_limit_bytes=32 * 1024 * 1024),
         cost_estimate=pl.CostEstimate(flops=500_000_000, bytes_accessed=3_000_000, transcendentals=100_000),
         name="finish",
-    )(even, live, side_a, side_b, rim, field, sums, proj, ws, wt, owners)
+    )(even, side_a, side_b, rim, field, sums, proj, ws, wt, placing)
 
 
 def local(latents, owners, live_counts, spatial_weight, temporal_weight, out_weight):
@@ -255,9 +260,11 @@
     send_a, send_b, xt, ws = prep(even, latents, spatial_weight)
     side_b = lax.ppermute(send_b, "tile", [(1, 2), (2, 1)])
     side_a = lax.ppermute(send_a, "tile", [(0, 1), (1, 0), (2, 3), (3, 2)])
-    rim, field, sums, wt, proj = main(xt, ws, temporal_weight, out_weight)
     rows = streams * 2 * 3
-    outgoing = finish(even, live_counts, side_a, side_b, rim, field, sums, proj, ws, wt, owners.reshape(1, groups), rows)
+    rim, field, sums, wt, proj, placing = main(
+        live_counts, xt, ws, temporal_weight, out_weight, owners.reshape(1, groups), rows
+    )
+    outgoing = finish(even, side_a, side_b, rim, field, sums, proj, ws, wt, placing)
     band_list = [6, 7, 5, 4, 3, 2, 1, 0]
     stream_list = list(range(streams // 2, streams)) + list(range(streams // 2))
     parity = lax.axis_index("band")

time: 46.9 us -> 46.9 us (level)
  no operation moved by 1% of the time
where the time goes in v5:
time: 46.9 us; the launch traced here: 46.5 us
  blocking collectives  26.7 us (57%)
  starting transfers between devices  10.7 us (23%)
  Pallas kernels  7.52 us (16%)
  other arithmetic  0.77 us (2%)
  between operations  0.75 us (2%)
    all_to_all x1, blocking collectives, local(): lax.all_to_all(outgoing, 'stream', split_axis=0, concat_axis=0, tiled=Tru...  15.9 us
    all_to_all x1, blocking collectives, local(): lax.all_to_all(got, 'band', split_axis=0, concat_axis=0, tiled=True, axis...  10.8 us
    ppermute x1, starting transfers between devices, local(): side_a = lax.ppermute(send_a, 'tile', [(0, 1), (1, 0), (2, 3), (3, 2)])  8.79 us
    pallas_call x1, Pallas kernels, main(): pl.pallas_call(main_kernel, out_shape=(jax.ShapeDtypeStruct((2, TW, width...  4.62 us
    pallas_call x1, Pallas kernels, prep(): pl.pallas_call(prep_kernel, out_shape=(jax.ShapeDtypeStruct((TW * width,...  2.03 us
    ppermute x1, starting transfers between devices, local(): side_b = lax.ppermute(send_b, 'tile', [(1, 2), (2, 1)])  1.92 us
  transfers between devices with their start and end apart: 2, of which 0 were waited for; matrix products, arithmetic and copies ran while one was open for 0% of the time, Pallas kernels for 10%

profile of v5, /device:TPU:1, one launch (start us, length us, event | category | flops | bytes accessed | tf_op | source)
XLA Modules:
  0.0 46.5 jit_solution(1688601586148377736)
XLA Ops:
  0.0 0.0 copy-start
  0.0 0.0 copy-start.1
  0.0 2.0 %prep.1 = (bf16[192,256]{1,0:T(8,128)(2,1)S(1)}, bf16[192,256]{1,0:T(8,128)(2,1)S(1)}, bf16[4,18,48,256]{3,2,1,0:T(8,128)(2,1)S(1)}, bf16[3,3,256,256]{3,2,1,0:T(8,128)(2,1)S(1)}) custom-call(s32[1]{0:T(128)} %bitcast.even_ref, bf16[24,128,256]{2,1,0:T(8,128)(2,1)} %bitcast.8, bf16[3,3,256,256]{3,2,1,0:T(8,128)(2,1)} %ws_ref.1), custom_call_target="tpu_custom_call" | custom-call | flops 400000000 | bytes 3200000 | tf_op jit(solution)/shard_map/prep/pallas_call | solution.py:85
  2.0 8.8 %collective-permute-start = (bf16[192,256]{1,0:T(8,128)(2,1)S(1)}, bf16[192,256]{1,0:T(8,128)(2,1)S(1)}, u32[]{:S(2)}, u32[]{:S(2)}) collective-permute-start(bf16[192,256]{1,0:T(8,128)(2,1)S(1)} %get-tuple-element.17), channel_id=1, source_target_pairs={{0,8},{8,0},{16,24},{24,16},{1,9},{9,1},{17,25},{25,17},{2,10},{10... | collective-permute-start | bytes 294920 | tf_op jit(solution)/shard_map/ppermute | solution.py:262
  10.8 1.9 %collective-permute-start.1 = (bf16[192,256]{1,0:T(8,128)(2,1)S(1)}, bf16[192,256]{1,0:T(8,128)(2,1)S(1)}, u32[]{:S(2)}, u32[]{:S(2)}) collective-permute-start(bf16[192,256]{1,0:T(8,128)(2,1)S(1)} %get-tuple-element.18), channel_id=1, source_target_pairs={{8,16},{16,8},{9,17},{17,9},{10,18},{18,10},{11,19},{19,11},{12,20... | collective-permute-start | bytes 294920 | tf_op jit(solution)/shard_map/ppermute | solution.py:261
  13.4 0.0 copy-done
  13.4 0.0 copy-done.1
  13.4 0.0 copy-start.2
  13.4 4.6 %main.1 = (f32[2,4,48,256]{3,2,1,0:T(8,128)S(1)}, bf16[2,4,48,256]{3,2,1,0:T(8,128)(2,1)S(1)}, f32[3,2,8,256]{3,2,1,0:T(8,128)S(1)}, bf16[3,256,256]{2,1,0:T(8,1...) custom-call(s32[1]{0:T(128)S(6)} %copy.10.live_ref, ...), custom_call_target="tpu_custom_call" | custom-call | flops 4499999744 | bytes 4500000 | tf_op jit(solution)/shard_map/main/pallas_call | solution.py:167
  18.1 0.0 copy-done.2
  18.1 0.0 collective-permute-done.a_ref
  18.1 0.0 collective-permute-done.1.b_ref
  18.1 0.9 %finish.1 = bf16[96,128]{1,0:T(8,128)(2,1)S(1)} custom-call(s32[1]{0:T(128)} %bitcast.even_ref, bf16[192,256]{1,0:T(8,128)(2,1)S(1)} %collective-permute-done.a_ref, bf16[192,256]{1,0:T(8,128)(2,1)S(1)} %collective-permute-done.1.b_ref, f32[2,4,48,256]{3,2,1,0:T(8,128)S(1)} %get-tuple-element.21.rim_ref, ...), custom_call_target="tpu_custom_call" | custom-call | flops 500000000 | bytes 3000000 | tf_op jit(solution)/shard_map/finish/pallas_call | solution.py:244
  19.0 15.9 %all_to_all.10 = bf16[48,2,128]{2,1,0:T(2,128)(2,1)S(1)} all-to-all(bf16[48,2,128]{2,1,0:T(2,128)(2,1)S(1)} %bitcast.6), channel_id=1, replica_groups={{256,288,320,352,384,416,448,480,0,32,64,96,128,160,192,224},{257,289,3..., dimensions={0} | all-to-all | bytes 49152 | tf_op jit(solution)/shard_map/all_to_all | solution.py:274
  35.0 10.8 %all_to_all.11 = bf16[8,96,128]{2,1,0:T(8,128)(2,1)S(1)} all-to-all(bf16[8,96,128]{2,1,0:T(8,128)(2,1)S(1)} %broadcast_in_dim.9), channel_id=1, replica_groups={{6,7,5,4,3,2,1,0},{14,15,13,12,11,10,9,8},{22,23,21,20,19,18,17,16},{30..., dimensions={0} | all-to-all | bytes 393216 | tf_op jit(solution)/shard_map/all_to_all | solution.py:280
  45.8 0.7 %multiply_reduce_fusion = f32[96,128]{1,0:T(8,128)} fusion(bf16[8,96,128]{2,1,0:T(8,128)(2,1)S(1)} %all_to_all.11, f32[8]{0:T(128)S(1)} %convert_multiply_fusion), kind=kLoop, calls=%fused_computation | loop fusion | flops 282624 | bytes 245792 | tf_op jit(solution)/shard_map/reduce_sum | solution.py:281
  (4 shorter events, 0.1 us)
Async XLA Ops:
  0.0 13.4 %copy-start = (bf16[3,256]{1,0:T(4,128)(2,1)S(1)}, bf16[3,256]{1,0:T(4,128)(2,1)}, u32[]{:S(2)}) copy-start(bf16[3,256]{1,0:T(4,128)(2,1)} %wo_ref.1) | copy-start | bytes 4612
  0.0 13.4 %copy-start.1 = (s32[24,1]{0,1:T(1,128)S(1)}, s32[24,1]{0,1:T(1,128)}, u32[]{:S(2)}) copy-start(s32[24,1]{0,1:T(1,128)} %param.8) | copy-start | bytes 292
  2.0 16.1 %collective-permute-start = (bf16[192,256]{1,0:T(8,128)(2,1)S(1)}, bf16[192,256]{1,0:T(8,128)(2,1)S(1)}, u32[]{:S(2)}, u32[]{:S(2)}) collective-permute-start(bf16[192,256]{1,0:T(8,128)(2,1)S(1)} %get-tuple-element.17), channel_id=1, source_target_pairs={{0,8},{8,0},{16,24},{24,16},{1,9},{9,1},{17,25},{25,17},{2,10},{10... | collective-permute-start | bytes 294920 | tf_op jit(solution)/shard_map/ppermute | solution.py:262
  10.8 7.3 %collective-permute-start.1 = (bf16[192,256]{1,0:T(8,128)(2,1)S(1)}, bf16[192,256]{1,0:T(8,128)(2,1)S(1)}, u32[]{:S(2)}, u32[]{:S(2)}) collective-permute-start(bf16[192,256]{1,0:T(8,128)(2,1)S(1)} %get-tuple-element.18), channel_id=1, source_target_pairs={{8,16},{16,8},{9,17},{17,9},{10,18},{18,10},{11,19},{19,11},{12,20... | collective-permute-start | bytes 294920 | tf_op jit(solution)/shard_map/ppermute | solution.py:261
  13.4 4.6 %copy-start.2 = (s32[8]{0:T(128)S(1)}, s32[8]{0:T(128)}, u32[]{:S(2)}) copy-start(s32[8]{0:T(128)} %constant.19.clone) | copy-start | bytes 100

commit v6 on v5

--- a/solution.py
+++ b/solution.py
@@ -274,11 +274,10 @@
     got = lax.all_to_all(
         outgoing, "stream", split_axis=0, concat_axis=0, tiled=True, axis_index_groups=[stream_list]
     )
-    half = streams * 3 // 2
-    got = jnp.concatenate([got[half:], got[:half]], axis=0).reshape(1, rows, CELLS)
-    got = lax.optimization_barrier(jnp.broadcast_to(got, (bands, rows, CELLS)))
+    got = lax.optimization_barrier(jnp.broadcast_to(got.reshape(1, rows, CELLS), (bands, rows, CELLS)))
     got = lax.all_to_all(got, "band", split_axis=0, concat_axis=0, tiled=True, axis_index_groups=[band_list])
-    frames = jnp.sum(got.astype(F32) * signs[:, None, None], axis=0)
+    got = got.reshape(bands, 2, rows // 2, CELLS)[:, ::-1].astype(F32)
+    frames = jnp.sum(got * signs[:, None, None, None], axis=0)
     return frames.reshape(streams * 2, 1, 3, CELLS)
 
 

time: 46.9 us -> 46.8 us (level)
  no operation moved by 1% of the time
where the time goes in v6:
time: 46.8 us; the launch traced here: 46.4 us
  blocking collectives  26.7 us (57%)
  starting transfers between devices  10.7 us (23%)
  Pallas kernels  7.52 us (16%)
  other arithmetic  0.74 us (2%)
  between operations  0.74 us (2%)
    all_to_all x1, blocking collectives, local(): lax.all_to_all(outgoing, 'stream', split_axis=0, concat_axis=0, tiled=Tru...  15.9 us
    all_to_all x1, blocking collectives, local(): lax.all_to_all(got, 'band', split_axis=0, concat_axis=0, tiled=True, axis...  10.8 us
    ppermute x1, starting transfers between devices, local(): side_a = lax.ppermute(send_a, 'tile', [(0, 1), (1, 0), (2, 3), (3, 2)])  8.79 us
    pallas_call x1, Pallas kernels, main(): pl.pallas_call(main_kernel, out_shape=(jax.ShapeDtypeStruct((2, TW, width...  4.62 us
    pallas_call x1, Pallas kernels, prep(): pl.pallas_call(prep_kernel, out_shape=(jax.ShapeDtypeStruct((TW * width,...  2.03 us
    ppermute x1, starting transfers between devices, local(): side_b = lax.ppermute(send_b, 'tile', [(1, 2), (2, 1)])  1.92 us
  transfers between devices with their start and end apart: 2, of which 0 were waited for; matrix products, arithmetic and copies ran while one was open for 0% of the time, Pallas kernels for 10%

profile of v6, /device:TPU:1, one launch (start us, length us, event | category | flops | bytes accessed | tf_op | source)
XLA Modules:
  0.0 46.4 jit_solution(13371857421327742349)
XLA Ops:
  0.0 0.0 copy-start
  0.0 0.0 copy-start.1
  0.0 2.0 %prep.1 = (bf16[192,256]{1,0:T(8,128)(2,1)S(1)}, bf16[192,256]{1,0:T(8,128)(2,1)S(1)}, bf16[4,18,48,256]{3,2,1,0:T(8,128)(2,1)S(1)}, bf16[3,3,256,256]{3,2,1,0:T(8,128)(2,1)S(1)}) custom-call(s32[1]{0:T(128)} %bitcast.even_ref, bf16[24,128,256]{2,1,0:T(8,128)(2,1)} %bitcast.9, bf16[3,3,256,256]{3,2,1,0:T(8,128)(2,1)} %ws_ref.1), custom_call_target="tpu_custom_call" | custom-call | flops 400000000 | bytes 3200000 | tf_op jit(solution)/shard_map/prep/pallas_call | solution.py:85
  2.0 8.8 %collective-permute-start = (bf16[192,256]{1,0:T(8,128)(2,1)S(1)}, bf16[192,256]{1,0:T(8,128)(2,1)S(1)}, u32[]{:S(2)}, u32[]{:S(2)}) collective-permute-start(bf16[192,256]{1,0:T(8,128)(2,1)S(1)} %get-tuple-element.17), channel_id=1, source_target_pairs={{0,8},{8,0},{16,24},{24,16},{1,9},{9,1},{17,25},{25,17},{2,10},{10... | collective-permute-start | bytes 294920 | tf_op jit(solution)/shard_map/ppermute | solution.py:262
  10.8 1.9 %collective-permute-start.1 = (bf16[192,256]{1,0:T(8,128)(2,1)S(1)}, bf16[192,256]{1,0:T(8,128)(2,1)S(1)}, u32[]{:S(2)}, u32[]{:S(2)}) collective-permute-start(bf16[192,256]{1,0:T(8,128)(2,1)S(1)} %get-tuple-element.18), channel_id=1, source_target_pairs={{8,16},{16,8},{9,17},{17,9},{10,18},{18,10},{11,19},{19,11},{12,20... | collective-permute-start | bytes 294920 | tf_op jit(solution)/shard_map/ppermute | solution.py:261
  13.4 0.0 copy-done
  13.4 0.0 copy-done.1
  13.4 0.0 copy-start.2
  13.4 4.6 %main.1 = (f32[2,4,48,256]{3,2,1,0:T(8,128)S(1)}, bf16[2,4,48,256]{3,2,1,0:T(8,128)(2,1)S(1)}, f32[3,2,8,256]{3,2,1,0:T(8,128)S(1)}, bf16[3,256,256]{2,1,0:T(8,1...) custom-call(s32[1]{0:T(128)S(6)} %copy.10.live_ref, ...), custom_call_target="tpu_custom_call" | custom-call | flops 4499999744 | bytes 4500000 | tf_op jit(solution)/shard_map/main/pallas_call | solution.py:167
  18.1 0.0 copy-done.2
  18.1 0.0 collective-permute-done.a_ref
  18.1 0.0 collective-permute-done.1.b_ref
  18.1 0.9 %finish.1 = bf16[96,128]{1,0:T(8,128)(2,1)S(1)} custom-call(s32[1]{0:T(128)} %bitcast.even_ref, bf16[192,256]{1,0:T(8,128)(2,1)S(1)} %collective-permute-done.a_ref, bf16[192,256]{1,0:T(8,128)(2,1)S(1)} %collective-permute-done.1.b_ref, f32[2,4,48,256]{3,2,1,0:T(8,128)S(1)} %get-tuple-element.21.rim_ref, ...), custom_call_target="tpu_custom_call" | custom-call | flops 500000000 | bytes 3000000 | tf_op jit(solution)/shard_map/finish/pallas_call | solution.py:244
  19.0 15.9 %all_to_all.10 = bf16[48,2,128]{2,1,0:T(2,128)(2,1)S(1)} all-to-all(bf16[48,2,128]{2,1,0:T(2,128)(2,1)S(1)} %bitcast.7), channel_id=1, replica_groups={{256,288,320,352,384,416,448,480,0,32,64,96,128,160,192,224},{257,289,3..., dimensions={0} | all-to-all | bytes 49152 | tf_op jit(solution)/shard_map/all_to_all | solution.py:274
  34.9 10.8 %all_to_all.11 = bf16[8,96,128]{2,1,0:T(8,128)(2,1)S(1)} all-to-all(bf16[8,96,128]{2,1,0:T(8,128)(2,1)S(1)} %broadcast_in_dim.9), channel_id=1, replica_groups={{6,7,5,4,3,2,1,0},{14,15,13,12,11,10,9,8},{22,23,21,20,19,18,17,16},{30..., dimensions={0} | all-to-all | bytes 393216 | tf_op jit(solution)/shard_map/all_to_all | solution.py:278
  45.7 0.7 %multiply_reduce_fusion = f32[2,48,128]{2,1,0:T(8,128)} fusion(f32[8]{0:T(128)S(1)} %convert_multiply_fusion, bf16[8,2,48,128]{3,2,1,0:T(8,128)(2,1)S(1)} %bitcast.10), kind=kLoop, calls=%fused_computation | loop fusion | flops 282624 | bytes 245792 | tf_op jit(solution)/shard_map/reduce_sum | solution.py:280
  (2 shorter events, 0.0 us)
Async XLA Ops:
  0.0 13.4 %copy-start = (bf16[3,256]{1,0:T(4,128)(2,1)S(1)}, bf16[3,256]{1,0:T(4,128)(2,1)}, u32[]{:S(2)}) copy-start(bf16[3,256]{1,0:T(4,128)(2,1)} %wo_ref.1) | copy-start | bytes 4612
  0.0 13.4 %copy-start.1 = (s32[24,1]{0,1:T(1,128)S(1)}, s32[24,1]{0,1:T(1,128)}, u32[]{:S(2)}) copy-start(s32[24,1]{0,1:T(1,128)} %param.8) | copy-start | bytes 292
  2.0 16.1 %collective-permute-start = (bf16[192,256]{1,0:T(8,128)(2,1)S(1)}, bf16[192,256]{1,0:T(8,128)(2,1)S(1)}, u32[]{:S(2)}, u32[]{:S(2)}) collective-permute-start(bf16[192,256]{1,0:T(8,128)(2,1)S(1)} %get-tuple-element.17), channel_id=1, source_target_pairs={{0,8},{8,0},{16,24},{24,16},{1,9},{9,1},{17,25},{25,17},{2,10},{10... | collective-permute-start | bytes 294920 | tf_op jit(solution)/shard_map/ppermute | solution.py:262
  10.8 7.3 %collective-permute-start.1 = (bf16[192,256]{1,0:T(8,128)(2,1)S(1)}, bf16[192,256]{1,0:T(8,128)(2,1)S(1)}, u32[]{:S(2)}, u32[]{:S(2)}) collective-permute-start(bf16[192,256]{1,0:T(8,128)(2,1)S(1)} %get-tuple-element.18), channel_id=1, source_target_pairs={{8,16},{16,8},{9,17},{17,9},{10,18},{18,10},{11,19},{19,11},{12,20... | collective-permute-start | bytes 294920 | tf_op jit(solution)/shard_map/ppermute | solution.py:261
  13.4 4.6 %copy-start.2 = (s32[8]{0:T(128)S(1)}, s32[8]{0:T(128)}, u32[]{:S(2)}) copy-start(s32[8]{0:T(128)} %constant.19.clone) | copy-start | bytes 100
